TPU v7x, 32 devices: a whole 2x2x4 slice. The times are simulated.
32 devices in a mesh: layer: 2 (over x), expert: 16 (over z, y, core).
Axes of the slice: x: 2, y: 2, z: 4, core: 2. Of those that a mesh axis runs over, the one named last changes fastest.
Arguments:
- grad_hidden: bfloat16 [8192, 384], P(('layer', 'expert')), parts along dimension 0, may hold values from -6 to 6
- grad_out: bfloat16 [8192, 1024], P(('layer', 'expert')), parts along dimension 0, may hold values from -0.41992188 to 0.41992188
- grad_route: int32 [8192, 1], P(('layer', 'expert')), parts along dimension 0, may hold values from 0 to 15; in each aligned block of 256 rows (0 to 255, 256 to 511, ...) at most 32 rows name the same one
- live_rows: int32 [32], P(('layer', 'expert')), parts along dimension 0, may hold values from 1 to 256, 3072 in all
- w_down: bfloat16 [32, 384, 1024], P(('layer', 'expert')), parts along dimension 0, may hold values from -0.3125 to 0.3125
- w_moment: bfloat16 [32, 384, 1024], P(('layer', 'expert')), parts along dimension 0, may hold values from -6 to 6
- perm: int32 [32], P('layer'), parts along dimension 0, may hold values from 0 to 15, each once
- fwd_hidden: bfloat16 [8192, 384], P(('layer', 'expert')), parts along dimension 0, may hold values from -6 to 6
- fwd_route: int32 [8192, 1], P(('layer', 'expert')), parts along dimension 0, may hold values from 0 to 15; in each aligned block of 256 rows (0 to 255, 256 to 511, ...) at most 32 rows name the same one
- fwd_gate: float32 [8192], P(('layer', 'expert')), parts along dimension 0, may hold values from 0.25 to 1
Outputs:
- placed_weight: bfloat16 [32, 384, 1024], P(('layer', 'expert')), parts along dimension 0
- placed_moment: bfloat16 [32, 384, 1024], P(('layer', 'expert')), parts along dimension 0
- fwd_out: bfloat16 [8192, 1024], P(('layer', 'expert')), parts along dimension 0
There are 2 independent parts, one for each index of `layer`. A program takes and returns all parts, laid end to end along the dimension named above; each array names one. Nothing has to cross between parts.
Inputs may be any that keep to these rules, and one draw needn't show every extreme that they name: `grad_route`: among the 256 rows of one device no expert is named more than 32 times, and in some device's rows some expert is named exactly 32 times. `fwd_route`: among the 256 rows of one device no expert is named more than 32 times, and in some device's rows some expert is named exactly 32 times. `live_rows`: within each layer the counts sum to three quarters of 4096, and some device has all 256 rows live. `perm`: each device number appears once.
All inputs are finite; a program needn't handle non-finite values.
Results may differ from a plain program's by a relative error of at most 0.0065.
Values may be sent and summed in bfloat16 or wider, within the bound.
No kernel may reach another device: no remote copies, remote signals or barrier semaphores. Data moves between devices by JAX's collectives and lax.ppermute only.
A program may use at most 64 MiB of HBM per device.

v0:
```python
import functools

import jax
import jax.numpy as jnp
from jax import lax
from jax.experimental import pallas as pl
from jax.experimental.pallas import tpu as pltpu
from jax.sharding import PartitionSpec as P

linear_term = 3.4445
cubic_term = -4.775
quintic_term = 2.0315
moment_decay = 0.9
step_scale = 0.25
norm_floor = 1e-07

F32 = jnp.float32
BF16 = jnp.bfloat16
HBM = pl.BlockSpec(memory_space=pltpu.HBM)
VMEM = pl.BlockSpec(memory_space=pltpu.VMEM)
SMEM = pl.BlockSpec(memory_space=pltpu.SMEM)
ANY = pl.BlockSpec(memory_space=pl.ANY)
MIB = 1 << 20


def row_block(k, rows):
    return pl.ds(pl.multiple_of(k * rows, rows), rows)


def crossing_ranks(half, base, perm_ref):
    flags = [(perm_ref[base + q] // half != base // half).astype(jnp.int32) for q in range(half)]
    ranks, count = [], 0
    for flag in flags:
        ranks.append(count)
        count = count + flag
    return flags, ranks


def slots_of(half):
    return half // 2, 1, half - half // 2 - 1


def slot_rows(route, live, groups, capacity, me_ref, perm_ref):
    rows = route.shape[1]
    experts = lax.broadcasted_iota(jnp.int32, (groups, rows), 0)
    onehot = jnp.where((experts == route) & live, 1.0, 0.0).astype(BF16)
    before = lax.broadcasted_iota(jnp.int32, (rows, rows), 0)
    after = lax.broadcasted_iota(jnp.int32, (rows, rows), 1)
    upto = jnp.where(before <= after, 1.0, 0.0).astype(BF16)
    ranks = jnp.dot(onehot, upto, preferred_element_type=F32)
    rank = jnp.sum(ranks * onehot.astype(F32), axis=0, keepdims=True).astype(jnp.int32) - 1
    partner = jnp.zeros_like(route)
    for e in range(groups):
        partner = jnp.where(route == e, perm_ref[e] ^ me_ref[0], partner)
    return jnp.where(live, partner * capacity + rank, -1)


def selector_of(slot, slots):
    rows = slot.shape[1]
    places = lax.broadcasted_iota(jnp.int32, (slots, rows), 0)
    return jnp.where(places == slot, 1.0, 0.0).astype(BF16)


def pack_kernel(groups, live_ref, me_ref, perm_ref, *refs):
    sources, pieces, (slot_ref, gates_ref) = refs[:6], refs[7 : 7 + groups], refs[7 + groups : 9 + groups]
    held, sem = refs[9 + groups : 15 + groups], refs[-1]
    route_ref, fwd_route_ref, hidden_ref, out_ref, fwd_ref, gate_ref = held
    copies = [pltpu.make_async_copy(ref, room, sem.at[n]) for n, (ref, room) in enumerate(zip(sources, held))]
    for copy in copies:
        copy.start()
    rows, ff = hidden_ref.shape
    d = out_ref.shape[1]
    capacity = pieces[0].shape[0]
    slots = groups * capacity
    place = lax.broadcasted_iota(jnp.int32, (1, rows), 1)

    def fill(first, selector, source_ref):
        chosen = jnp.dot(selector, source_ref[...], preferred_element_type=F32).astype(BF16)
        for s, piece in zip(mixed_order(groups), pieces):
            piece[:, first : first + source_ref.shape[1]] = chosen[s * capacity : (s + 1) * capacity]

    copies[0].wait()
    slot = slot_rows(route_ref[...], place < live_ref[0], groups, capacity, me_ref, perm_ref)
    selector = selector_of(slot, slots)
    copies[1].wait()
    fwd_slot = slot_rows(fwd_route_ref[...], place >= 0, groups, capacity, me_ref, perm_ref)
    slot_ref[...] = fwd_slot
    copies[2].wait()
    fill(0, selector, hidden_ref)
    copies[3].wait()
    fill(ff, selector, out_ref)
    copies[4].wait()
    fill(ff + d, selector_of(fwd_slot, slots), fwd_ref)
    copies[5].wait()
    down = lax.broadcasted_iota(jnp.int32, (rows, rows), 0)
    across = lax.broadcasted_iota(jnp.int32, (rows, rows), 1)
    gates_ref[...] = jnp.sum(jnp.where(down == across, gate_ref[...], 0.0), axis=1, keepdims=True)


def pack_rows(live_rows, me, perm, route, fwd_route, hidden, grad_out, fwd_hidden, gate, earlier, groups, capacity):
    rows, ff = hidden.shape
    width = 2 * ff + grad_out.shape[1]
    sources = (route.reshape(1, rows), fwd_route.reshape(1, rows), hidden, grad_out, fwd_hidden, gate.reshape(1, rows))
    *pieces, slot, gates = pl.pallas_call(
        functools.partial(pack_kernel, groups),
        out_shape=(jax.ShapeDtypeStruct((capacity, width), BF16),) * groups
        + (jax.ShapeDtypeStruct((1, rows), jnp.int32), jax.ShapeDtypeStruct((rows, 1), F32)),
        in_specs=[SMEM] * 3 + [HBM] * 6 + [VMEM],
        out_specs=(VMEM,) * (groups + 2),
        scratch_shapes=[pltpu.VMEM(a.shape, a.dtype) for a in sources] + [pltpu.SemaphoreType.DMA((len(sources),))],
        compiler_params=pltpu.CompilerParams(vmem_limit_bytes=32 * MIB),
        cost_estimate=pl.CostEstimate(
            flops=2 * groups * capacity * rows * width, bytes_accessed=6 * rows * width, transcendentals=0
        ),
        name="pack_rows",
    )(live_rows, me, perm, *sources, earlier)
    return pieces, slot, gates


def split_kernel(me_ref, matrix_ref, *refs):
    pieces, sem = refs[1:-1], refs[-1]
    half, rows = len(pieces), pieces[0].shape[0]
    copies = [
        pltpu.make_async_copy(matrix_ref.at[0, row_block((me_ref[0] ^ s) % half, rows)], piece, sem.at[s])
        for s, piece in zip(return_order(half), pieces)
    ]
    for copy in copies:
        copy.start()
    for copy in copies:
        copy.wait()


def split(me, matrix, earlier, half):
    _, ff, d = matrix.shape
    piece = jax.ShapeDtypeStruct((ff // half, d), BF16)
    return pl.pallas_call(
        split_kernel,
        out_shape=(piece,) * half,
        in_specs=[SMEM, HBM, VMEM],
        out_specs=(VMEM,) * half,
        scratch_shapes=[pltpu.SemaphoreType.DMA((half,))],
        compiler_params=pltpu.CompilerParams(vmem_limit_bytes=60 * MIB),
        cost_estimate=pl.CostEstimate(flops=0, bytes_accessed=4 * ff * d, transcendentals=0),
        name="split",
    )(me, matrix, earlier)


def sort_kernel(me_ref, perm_ref, *refs):
    pieces, (near_ref, *slot_refs) = refs[:-4], refs[-4:]
    half = len(pieces)
    me = me_ref[0]
    base = me // half * half
    flags, ranks = crossing_ranks(half, base, perm_ref)
    for s, piece in zip(return_order(half), pieces):
        place = (me ^ s) % half
        crosses, rank = 0, 0
        for q in range(half):
            crosses = jnp.where(place == q, flags[q], crosses)
            rank = jnp.where(place == q, ranks[q], rank)
        near = (perm_ref[base + place] ^ me) % half

        @pl.when(crosses == 0)
        def _():
            near_ref[near] = piece[...]

        first = 0
        for slots in slot_refs:
            count = slots.shape[0]

            @pl.when((crosses == 1) & (rank >= first) & (rank < first + count))
            def _():
                slots[rank - first] = piece[...]

            first += count


def sort_pieces(me, perm, pieces):
    half = len(pieces)
    shape = pieces[0].shape
    counts = (half,) + slots_of(half)
    return pl.pallas_call(
        sort_kernel,
        out_shape=tuple(jax.ShapeDtypeStruct((count,) + shape, BF16) for count in counts),
        in_specs=[SMEM, SMEM] + [VMEM] * half,
        out_specs=(VMEM,) * len(counts),
        compiler_params=pltpu.CompilerParams(vmem_limit_bytes=32 * MIB),
        cost_estimate=pl.CostEstimate(flops=0, bytes_accessed=4 * half * pieces[0].size, transcendentals=0),
        name="sort_pieces",
    )(me, perm, *pieces)


def join_kernel(half, me_ref, perm_ref, near_ref, *refs):
    slot_refs, targets = refs[:3], refs[3:]
    me = me_ref[0]
    base = me // half * half
    flags, ranks = crossing_ranks(half, half - base, perm_ref)
    for s, target in zip(return_order(half), targets):
        crosses, rank = 0, 0
        for q in range(half):
            here = perm_ref[half - base + q] == me ^ s
            crosses = jnp.where(here, 1, crosses)
            rank = jnp.where(here, ranks[q], rank)

        @pl.when(crosses == 0)
        def _():
            target[...] = near_ref[s]

        first = 0
        for slots in slot_refs:
            count = slots.shape[0]

            @pl.when((crosses == 1) & (rank >= first) & (rank < first + count))
            def _():
                target[...] = slots[rank - first]

            first += count


def join_pieces(me, perm, near, slots):
    half = near.shape[0]
    piece = jax.ShapeDtypeStruct(near.shape[1:], BF16)
    return pl.pallas_call(
        functools.partial(join_kernel, half),
        out_shape=(piece,) * half,
        in_specs=[SMEM, SMEM] + [VMEM] * 4,
        out_specs=(VMEM,) * half,
        compiler_params=pltpu.CompilerParams(vmem_limit_bytes=32 * MIB),
        cost_estimate=pl.CostEstimate(flops=0, bytes_accessed=4 * near.size, transcendentals=0),
        name="join_pieces",
    )(me, perm, near, *slots)


def gradient_kernel(groups, *refs):
    pieces, (grad_ref, fwd_ref, rows_ref) = refs[:groups], refs[groups:]
    ff, d = grad_ref.shape
    capacity = pieces[0].shape[0]
    for n, piece in enumerate(pieces):
        span = slice(n * capacity, (n + 1) * capacity)
        rows_ref[span] = piece[:, : ff + d]
        fwd_ref[span] = piece[:, ff + d :]
    grad_ref[...] = lax.dot_general(
        rows_ref[:, :ff], rows_ref[:, ff:], (((0,), (0,)), ((), ())), preferred_element_type=F32
    )


def gradient(pieces, ff, d):
    groups = len(pieces)
    slots = groups * pieces[0].shape[0]
    return pl.pallas_call(
        functools.partial(gradient_kernel, groups),
        out_shape=(jax.ShapeDtypeStruct((ff, d), F32), jax.ShapeDtypeStruct((slots, ff), BF16)),
        in_specs=[VMEM] * groups,
        out_specs=(VMEM, VMEM),
        scratch_shapes=[pltpu.VMEM((slots, ff + d), BF16)],
        compiler_params=pltpu.CompilerParams(vmem_limit_bytes=32 * MIB),
        cost_estimate=pl.CostEstimate(
            flops=2 * ff * d * slots, bytes_accessed=4 * ff * d + 4 * slots * (ff + d), transcendentals=0
        ),
        name="gradient",
    )(*pieces)


def assembled(me_ref, pieces, held):
    half, rows = len(pieces), pieces[0].shape[0]
    for s, piece in zip(return_order(half), pieces):
        held[row_block((me_ref[0] ^ s) % half, rows)] = piece[...]
    return held[...].astype(F32)


def orthogonal_kernel(me_ref, grad_ref, *refs):
    pieces, (moment_new_ref, ortho_ref, held) = refs[:-3], refs[-3:]
    moment_new = (moment_decay * assembled(me_ref, pieces, held) + grad_ref[...]).astype(BF16)
    moment_new_ref[...] = moment_new
    moment_f = moment_new.astype(F32)
    frobenius = jnp.sqrt(jnp.sum(moment_f * moment_f))
    current = (moment_f / (frobenius + norm_floor)).astype(BF16)
    for _ in range(2):
        gramian = lax.dot_general(
            current, current, (((1,), (1,)), ((), ())), preferred_element_type=F32
        ).astype(BF16)
        squared = jnp.dot(gramian, gramian, preferred_element_type=F32)
        poly = (cubic_term * gramian.astype(F32) + quintic_term * squared).astype(BF16)
        current = (
            linear_term * current.astype(F32) + jnp.dot(poly, current, preferred_element_type=F32)
        ).astype(BF16)
    ortho_ref[...] = current


def orthogonal(me, grad, pieces):
    ff, d = grad.shape
    shape = jax.ShapeDtypeStruct((ff, d), BF16)
    return pl.pallas_call(
        orthogonal_kernel,
        out_shape=(shape, shape),
        in_specs=[SMEM, VMEM] + [VMEM] * len(pieces),
        out_specs=(VMEM, VMEM),
        scratch_shapes=[pltpu.VMEM((ff, d), BF16)],
        compiler_params=pltpu.CompilerParams(vmem_limit_bytes=32 * MIB),
        cost_estimate=pl.CostEstimate(
            flops=8 * ff * ff * d + 4 * ff**3, bytes_accessed=10 * ff * d, transcendentals=1
        ),
        name="orthogonal",
    )(me, grad, *pieces)


def produce_kernel(half, me_ref, ortho_ref, fwd_ref, *refs):
    pieces, (weight_new_ref, *produced), held = refs[:half], refs[half:-1], refs[-1]
    weight = assembled(me_ref, pieces, held)
    weight_new = (weight - step_scale * ortho_ref[...].astype(F32)).astype(BF16)
    weight_new_ref[...] = weight_new
    product = jnp.dot(fwd_ref[...], weight_new, preferred_element_type=F32).astype(BF16)
    groups, capacity = len(produced), produced[0].shape[0]
    came = mixed_order(groups)
    for s, piece in zip(return_order(groups), produced):
        n = came.index(s)
        piece[...] = product[n * capacity : (n + 1) * capacity]


def produce(me, ortho, fwd_rows, pieces, groups):
    half = len(pieces)
    ff, d = ortho.shape
    slots = fwd_rows.shape[0]
    weight_new, *produced = pl.pallas_call(
        functools.partial(produce_kernel, half),
        out_shape=(jax.ShapeDtypeStruct((ff, d), BF16),)
        + (jax.ShapeDtypeStruct((slots // groups, d), BF16),) * groups,
        in_specs=[SMEM] + [VMEM] * (2 + half),
        out_specs=(VMEM,) * (groups + 1),
        scratch_shapes=[pltpu.VMEM((ff, d), BF16)],
        compiler_params=pltpu.CompilerParams(vmem_limit_bytes=32 * MIB),
        cost_estimate=pl.CostEstimate(
            flops=2 * ff * d * slots, bytes_accessed=8 * ff * d + 2 * slots * (ff + d), transcendentals=0
        ),
        name="produce",
    )(me, ortho, fwd_rows, *pieces)
    return weight_new, produced


def finish_kernel(groups, slot_ref, gates_ref, *refs):
    pieces, (out_ref, returned_ref) = refs[:groups], refs[groups:]
    capacity = pieces[0].shape[0]
    for s, piece in zip(return_order(groups), pieces):
        returned_ref[s * capacity : (s + 1) * capacity] = piece[...]
    selector = selector_of(slot_ref[...], groups * capacity)
    expert_out = lax.dot_general(
        selector, returned_ref[...], (((0,), (0,)), ((), ())), preferred_element_type=F32
    )
    out_ref[...] = (gates_ref[...] * expert_out).astype(BF16)


def finish(slot, gates, returned):
    groups = len(returned)
    rows = slot.shape[1]
    capacity, d = returned[0].shape
    slots = groups * capacity
    return pl.pallas_call(
        functools.partial(finish_kernel, groups),
        out_shape=jax.ShapeDtypeStruct((rows, d), BF16),
        in_specs=[VMEM] * (2 + groups),
        out_specs=VMEM,
        scratch_shapes=[pltpu.VMEM((slots, d), BF16)],
        compiler_params=pltpu.CompilerParams(vmem_limit_bytes=32 * MIB),
        cost_estimate=pl.CostEstimate(
            flops=2 * slots * rows * d, bytes_accessed=2 * d * (slots + rows), transcendentals=0
        ),
        name="finish",
    )(slot, gates, *returned)


def mixed_order(groups):
    far, near = list(range(groups // 2, groups)), list(range(groups // 2 - 1, 0, -1))
    return [0] + [s for pair in zip(far, near + [None]) for s in pair if s is not None]


def return_order(groups):
    far, near = list(range(groups // 2, groups)), list(range(groups // 2 - 1, 0, -1))
    order = [0]
    while far or near:
        order += far[:2] + near[:1]
        far, near = far[2:], near[1:]
    return order


def swap(pieces, order):
    groups = lax.axis_size("expert")
    return [
        lax.ppermute(piece, "expert", [(i, i ^ s) for i in range(groups)]) if s else piece
        for s, piece in zip(order, pieces)
    ]


def halves_plan(
    grad_hidden, grad_out, grad_route, live_rows, w_down, w_moment, perm, fwd_hidden, fwd_route, fwd_gate
):
    groups = lax.axis_size("expert")
    layers = lax.axis_size("layer")
    half = groups // 2
    me = lax.axis_index("expert").astype(jnp.int32).reshape(1)
    capacity = max(4, 2 * grad_hidden.shape[0] // groups)
    ff, d = w_down.shape[1:]
    crossing = jnp.sum((perm[:half] >= half).astype(jnp.int32)).reshape(1)
    most = crossing
    for turn in range(1, layers):
        other = lax.ppermute(crossing, "layer", [(i, (i + turn) % layers) for i in range(layers)])
        most = jnp.maximum(most, other)
    most = most[0]

    near_order, slot_counts = return_order(half), slots_of(half)

    def mirror(array):
        return swap([array], [half])[0]

    def gathered(spread):
        near, first, following, rest = sort_pieces(me, perm, spread)
        crossed = [
            mirror(first),
            lax.cond(most > slot_counts[0], mirror, lambda array: array, following),
            lax.cond(most > slot_counts[0] + slot_counts[1], mirror, lambda array: array, rest),
        ]
        return swap(join_pieces(me, perm, near, crossed), near_order)

    moment_pieces = split(me, w_moment, live_rows, half)
    packed, fwd_slot, gates = pack_rows(
        live_rows, me, perm, grad_route, fwd_route, grad_hidden, grad_out, fwd_hidden, fwd_gate,
        moment_pieces[0], groups, capacity,
    )
    weight_pieces = split(me, w_down, fwd_slot, half)
    received = swap(packed, mixed_order(groups))
    moment_placed = gathered(swap(moment_pieces, near_order))
    weight_placed = gathered(swap(weight_pieces, near_order))
    grad, fwd_rows = gradient(received, ff, d)
    moment_new, ortho = orthogonal(me, grad, moment_placed)
    weight_new, produced = produce(me, ortho, fwd_rows, weight_placed, groups)
    returned = swap(produced, return_order(groups))
    return weight_new[None], moment_new[None], finish(fwd_slot, gates, returned)


def lookup(route_ids, mapping):
    columns = jnp.arange(mapping.shape[0], dtype=jnp.int32)
    hits = route_ids[:, None] == columns[None, :]
    return jnp.sum(jnp.where(hits, mapping[None, :], 0), axis=1)


def slot_matrix(target, is_live, groups, capacity):
    columns = jnp.arange(groups, dtype=jnp.int32)
    onehot = ((target[:, None] == columns[None, :]) & is_live[:, None]).astype(jnp.int32)
    ranked = jnp.sum(jnp.cumsum(onehot, axis=0) * onehot, axis=1) - 1
    slot_of = jnp.where(is_live, target * capacity + ranked, -1)
    slots = jnp.arange(groups * capacity, dtype=jnp.int32)
    return (slots[:, None] == slot_of[None, :]).astype(jnp.bfloat16)


def orthogonalize(moment):
    moment_f = moment.astype(jnp.float32)
    frobenius = jnp.sqrt(jnp.sum(moment_f * moment_f))
    current = (moment_f / (frobenius + norm_floor)).astype(jnp.bfloat16)
    for sweep_index in range(2):
        gramian = lax.dot_general(
            current, current, (((1,), (1,)), ((), ())), preferred_element_type=jnp.float32
        ).astype(jnp.bfloat16)
        squared = jnp.dot(gramian, gramian, preferred_element_type=jnp.float32)
        poly = (cubic_term * gramian.astype(jnp.float32) + quintic_term * squared).astype(
            jnp.bfloat16
        )
        current = (
            linear_term * current.astype(jnp.float32)
            + jnp.dot(poly, current, preferred_element_type=jnp.float32)
        ).astype(jnp.bfloat16)
    return current


def relocate(weight, moment, perm):
    groups = lax.axis_size("expert")
    weight_flat = weight.reshape(groups, -1)
    moment_flat = moment.reshape(groups, -1)
    spread_w, spread_m = (
        lax.all_to_all(weight_flat, "expert", split_axis=0, concat_axis=0, tiled=True),
        lax.all_to_all(moment_flat, "expert", split_axis=0, concat_axis=0, tiled=True),
    )
    devices = jnp.arange(groups, dtype=jnp.int32)
    inverse = jnp.sum(jnp.where(perm[None, :] == devices[:, None], devices[None, :], 0), axis=1)
    ordered_w = jnp.take(spread_w, inverse, axis=0)
    ordered_m = jnp.take(spread_m, inverse, axis=0)
    back_w, back_m = (
        lax.all_to_all(ordered_w, "expert", split_axis=0, concat_axis=0, tiled=True),
        lax.all_to_all(ordered_m, "expert", split_axis=0, concat_axis=0, tiled=True),
    )
    return (back_w.reshape(weight.shape), back_m.reshape(moment.shape))


def routed_plan(
    grad_hidden,
    grad_out,
    grad_route,
    live_rows,
    w_down,
    w_moment,
    perm,
    fwd_hidden,
    fwd_route,
    fwd_gate,
):
    groups = lax.axis_size("expert")
    grad_count = grad_hidden.shape[0]
    capacity = max(4, 2 * grad_count // groups)
    is_live = jnp.arange(grad_count, dtype=jnp.int32) < live_rows[0]
    route_ids = grad_route[:, 0]
    weight, moment = relocate(w_down, w_moment, perm)
    target = lookup(route_ids, perm)
    selector = slot_matrix(target, is_live, groups, capacity)
    hidden_buf = (
        jnp.dot(selector, grad_hidden, preferred_element_type=jnp.float32)
        .astype(jnp.bfloat16)
        .reshape(groups, capacity, -1)
    )
    outgrad_buf = (
        jnp.dot(selector, grad_out, preferred_element_type=jnp.float32)
        .astype(jnp.bfloat16)
        .reshape(groups, capacity, -1)
    )
    recv_hidden, recv_outgrad = (
        lax.all_to_all(hidden_buf, "expert", split_axis=0, concat_axis=0, tiled=True),
        lax.all_to_all(outgrad_buf, "expert", split_axis=0, concat_axis=0, tiled=True),
    )
    grad = lax.dot_general(
        recv_hidden.reshape(groups * capacity, -1),
        recv_outgrad.reshape(groups * capacity, -1),
        (((0,), (0,)), ((), ())),
        preferred_element_type=jnp.float32,
    )
    moment_new = (moment_decay * moment[0].astype(jnp.float32) + grad).astype(jnp.bfloat16)
    ortho = orthogonalize(moment_new)
    weight_new = (weight[0].astype(jnp.float32) - step_scale * ortho.astype(jnp.float32)).astype(
        jnp.bfloat16
    )
    weight_new = weight_new[None]
    moment_new = moment_new[None]
    fwd_ids = fwd_route[:, 0]
    placed_weight, placed_moment = (weight_new, moment_new)
    fwd_target = lookup(fwd_ids, perm)
    fwd_weight = weight_new[0]
    fwd_count = fwd_hidden.shape[0]
    fwd_capacity = max(4, 2 * fwd_count // groups)
    fwd_selector = slot_matrix(fwd_target, jnp.ones((fwd_count,), dtype=bool), groups, fwd_capacity)
    fwd_buf = (
        jnp.dot(fwd_selector, fwd_hidden, preferred_element_type=jnp.float32)
        .astype(jnp.bfloat16)
        .reshape(groups, fwd_capacity, -1)
    )
    produced = jnp.einsum(
        "gkf,fd->gkd",
        lax.all_to_all(fwd_buf, "expert", split_axis=0, concat_axis=0, tiled=True),
        fwd_weight,
        preferred_element_type=jnp.float32,
    ).astype(jnp.bfloat16)
    returned = lax.all_to_all(produced, "expert", split_axis=0, concat_axis=0, tiled=True)
    fwd_rows_out = lax.dot_general(
        fwd_selector,
        returned.reshape(groups * fwd_capacity, -1),
        (((0,), (0,)), ((), ())),
        preferred_element_type=jnp.float32,
    )
    fwd_out = (fwd_rows_out * fwd_gate[:, None]).astype(jnp.bfloat16)
    return (placed_weight, placed_moment, fwd_out)


def solution(mesh):
    groups = mesh.shape["expert"]
    in_specs = (
        P(("layer", "expert"), None),
        P(("layer", "expert"), None),
        P(("layer", "expert"), None),
        P(("layer", "expert")),
        P(("layer", "expert"), None, None),
        P(("layer", "expert"), None, None),
        P("layer"),
        P(("layer", "expert"), None),
        P(("layer", "expert"), None),
        P(("layer", "expert")),
    )
    out_specs = (
        P(("layer", "expert"), None, None),
        P(("layer", "expert"), None, None),
        P(("layer", "expert"), None),
    )

    def per_device(*args):
        few = groups >= 8 and groups & (groups - 1) == 0 and groups <= 2 * args[0].shape[0] // groups
        return (halves_plan if few else routed_plan)(*args)

    return jax.shard_map(
        per_device, mesh=mesh, in_specs=in_specs, out_specs=out_specs, check_vma=False
    )
```

profile of v0, /device:TPU:0, one launch (start us, length us, event | category | flops | bytes accessed | tf_op | source)
XLA Modules:
  0.0 177.8 jit_solution(11395041851366882953)
XLA Ops:
  1.3 2.2 %split.2 = (bf16[48,1024]{1,0:T(8,128)(2,1)}, bf16[48,1024]{1,0:T(8,128)(2,1)}, bf16[48,1024]{1,0:T(8,128)(2,1)}, bf16[48,1024]{1,0:T(8,128)(2,1)}, bf16[48,1024...) custom-call(s32[1]{0:T(128)} %bitcast.me_ref, ...), custom_call_target="tpu_custom_call" | custom-call | bytes 1572864 | tf_op jit(solution)/shard_map/split/pallas_call | solution.py:136
  3.5 3.1 %collective-permute-start.19 = (bf16[48,1024]{1,0:T(8,128)(2,1)}, bf16[48,1024]{1,0:T(8,128)(2,1)S(1)}, u32[]{:S(2)}, u32[]{:S(2)}) collective-permute-start(bf16[48,1024]{1,0:T(8,128)(2,1)} %get-tuple-element.120), channel_id=1, source_target_pairs={{0,4},{1,5},{2,6},{3,7},{4,0},{5,1},{6,2},{7,3},{8,12},{9,13},{10,... | collective-permute-start | bytes 294920 | tf_op jit(solution)/shard_map/ppermute | solution.py:387
  6.5 1.7 collective-permute-start.21
  12.6 2.2 %collective-permute-done.27 = s32[1]{0:T(128)} collective-permute-done((s32[1]{0:T(128)}, s32[1]{0:T(128)}, u32[]{:S(2)}, u32[]{:S(2)}) %collective-permute-start.27) | collective-permute-done | bytes 36 | tf_op jit(solution)/shard_map/ppermute | solution.py:404
  22.9 3.4 %pack_rows.1 = (bf16[32,1792]{1,0:T(8,128)(2,1)S(1)}, bf16[32,1792]{1,0:T(8,128)(2,1)}, bf16[32,1792]{1,0:T(8,128)(2,1)}, bf16[32,1792]{1,0:T(8,128)(2,1)}, bf16...) custom-call(s32[1]{0:T(128)S(6)} %copy.21.refs_0_.live_ref, ...), custom_call_target="tpu_custom_call" | custom-call | flops 469762048 | bytes 2752512 | tf_op jit(solution)/shard_map/pack_rows/pallas_call | solution.py:104
  33.9 2.8 %split.3 = (bf16[48,1024]{1,0:T(8,128)(2,1)}, bf16[48,1024]{1,0:T(8,128)(2,1)}, bf16[48,1024]{1,0:T(8,128)(2,1)}, bf16[48,1024]{1,0:T(8,128)(2,1)}, bf16[48,1024...) custom-call(s32[1]{0:T(128)} %bitcast.me_ref, ...), custom_call_target="tpu_custom_call" | custom-call | bytes 1572864 | tf_op jit(solution)/shard_map/split/pallas_call | solution.py:136
  36.7 1.8 %collective-permute-start.35 = (bf16[48,1024]{1,0:T(8,128)(2,1)}, bf16[48,1024]{1,0:T(8,128)(2,1)S(1)}, u32[]{:S(2)}, u32[]{:S(2)}) collective-permute-start(bf16[48,1024]{1,0:T(8,128)(2,1)} %get-tuple-element.143), channel_id=1, source_target_pairs={{0,4},{1,5},{2,6},{3,7},{4,0},{5,1},{6,2},{7,3},{8,12},{9,13},{10,... | collective-permute-start | bytes 294920 | tf_op jit(solution)/shard_map/ppermute | solution.py:387
  43.1 1.7 sort_pieces.2
  46.4 2.7 %collective-permute-start.4 = (bf16[32,1792]{1,0:T(8,128)(2,1)}, bf16[32,1792]{1,0:T(8,128)(2,1)S(1)}, u32[]{:S(2)}, u32[]{:S(2)}) collective-permute-start(bf16[32,1792]{1,0:T(8,128)(2,1)} %get-tuple-element.104), channel_id=1, source_target_pairs={{0,8},{1,9},{2,10},{3,11},{4,12},{5,13},{6,14},{7,15},{8,0},{9,1},... | collective-permute-start | bytes 344072 | tf_op jit(solution)/shard_map/ppermute | solution.py:387
  49.1 1.9 %collective-permute-start.5 = (bf16[32,1792]{1,0:T(8,128)(2,1)}, bf16[32,1792]{1,0:T(8,128)(2,1)S(1)}, u32[]{:S(2)}, u32[]{:S(2)}) collective-permute-start(bf16[32,1792]{1,0:T(8,128)(2,1)} %get-tuple-element.105), channel_id=1, source_target_pairs={{0,7},{1,6},{2,5},{3,4},{4,3},{5,2},{6,1},{7,0},{8,15},{9,14},{10,... | collective-permute-start | bytes 344072 | tf_op jit(solution)/shard_map/ppermute | solution.py:387
  51.1 2.0 %collective-permute-start.6 = (bf16[32,1792]{1,0:T(8,128)(2,1)}, bf16[32,1792]{1,0:T(8,128)(2,1)S(1)}, u32[]{:S(2)}, u32[]{:S(2)}) collective-permute-start(bf16[32,1792]{1,0:T(8,128)(2,1)} %get-tuple-element.106), channel_id=1, source_target_pairs={{0,9},{1,8},{2,11},{3,10},{4,13},{5,12},{6,15},{7,14},{8,1},{9,0},... | collective-permute-start | bytes 344072 | tf_op jit(solution)/shard_map/ppermute | solution.py:387
  55.4 1.7 sort_pieces.3
  57.2 5.0 %collective-permute-start.8 = (bf16[32,1792]{1,0:T(8,128)(2,1)}, bf16[32,1792]{1,0:T(8,128)(2,1)S(1)}, u32[]{:S(2)}, u32[]{:S(2)}) collective-permute-start(bf16[32,1792]{1,0:T(8,128)(2,1)} %copy-done.20), channel_id=1, source_target_pairs={{0,10},{1,11},{2,8},{3,9},{4,14},{5,15},{6,12},{7,13},{8,2},{9,3},... | collective-permute-start | bytes 344072 | tf_op jit(solution)/shard_map/ppermute | solution.py:387
  62.2 2.9 %collective-permute-start.42 = (bf16[4,48,1024]{2,1,0:T(8,128)(2,1)S(1)}, bf16[4,48,1024]{2,1,0:T(8,128)(2,1)S(1)}, u32[]{:S(2)}, u32[]{:S(2)}) collective-permute-start(bf16[4,48,1024]{2,1,0:T(8,128)(2,1)S(1)} %get-tuple-element.151), channel_id=1, source_target_pairs={{0,8},{1,9},{2,10},{3,11},{4,12},{5,13},{6,14},{7,15},{8,0},{9,1},... | collective-permute-start | bytes 1179656 | tf_op jit(solution)/shard_map/ppermute | solution.py:387
  65.6 19.9 %collective-permute-done.8.refs_5_ = bf16[32,1792]{1,0:T(8,128)(2,1)S(1)} collective-permute-done((bf16[32,1792]{1,0:T(8,128)(2,1)}, bf16[32,1792]{1,0:T(8,128)(2,1)S(1)}, u32[]{:S(2)}, u32[]{:S(2)}) %collective-permute-start.8) | collective-permute-done | bytes 114720 | tf_op jit(solution)/shard_map/ppermute | solution.py:387
  85.5 2.9 %collective-permute-start.12 = (bf16[32,1792]{1,0:T(8,128)(2,1)}, bf16[32,1792]{1,0:T(8,128)(2,1)S(1)}, u32[]{:S(2)}, u32[]{:S(2)}) collective-permute-start(bf16[32,1792]{1,0:T(8,128)(2,1)} %copy-done.16), channel_id=1, source_target_pairs={{0,12},{1,13},{2,14},{3,15},{4,8},{5,9},{6,10},{7,11},{8,4},{9,5},... | collective-permute-start | bytes 344072 | tf_op jit(solution)/shard_map/ppermute | solution.py:387
  88.4 20.7 %collective-permute-done.10.refs_7_ = bf16[32,1792]{1,0:T(8,128)(2,1)S(1)} collective-permute-done((bf16[32,1792]{1,0:T(8,128)(2,1)}, bf16[32,1792]{1,0:T(8,128)(2,1)S(1)}, u32[]{:S(2)}, u32[]{:S(2)}) %collective-permute-start.10) | collective-permute-done | bytes 114720 | tf_op jit(solution)/shard_map/ppermute | solution.py:387
  112.8 1.6 collective-permute-done.13.refs_10_
  116.0 2.4 %collective-permute-done.14.refs_11_ = bf16[32,1792]{1,0:T(8,128)(2,1)S(1)} collective-permute-done((bf16[32,1792]{1,0:T(8,128)(2,1)}, bf16[32,1792]{1,0:T(8,128)(2,1)S(1)}, u32[]{:S(2)}, u32[]{:S(2)}) %collective-permute-start.14) | collective-permute-done | bytes 114720 | tf_op jit(solution)/shard_map/ppermute | solution.py:387
  118.5 2.0 %collective-permute-start.18 = (bf16[32,1792]{1,0:T(8,128)(2,1)}, bf16[32,1792]{1,0:T(8,128)(2,1)S(1)}, u32[]{:S(2)}, u32[]{:S(2)}) collective-permute-start(bf16[32,1792]{1,0:T(8,128)(2,1)} %copy-done.10), channel_id=1, source_target_pairs={{0,15},{1,14},{2,13},{3,12},{4,11},{5,10},{6,9},{7,8},{8,7},{9,6},... | collective-permute-start | bytes 344072 | tf_op jit(solution)/shard_map/ppermute | solution.py:387
  127.0 2.5 %collective-permute-start.32 = (bf16[48,1024]{1,0:T(8,128)(2,1)S(1)}, bf16[48,1024]{1,0:T(8,128)(2,1)S(1)}, u32[]{:S(2)}, u32[]{:S(2)}) collective-permute-start(bf16[48,1024]{1,0:T(8,128)(2,1)S(1)} %get-tuple-element.136), channel_id=1, source_target_pairs={{0,7},{1,6},{2,5},{3,4},{4,3},{5,2},{6,1},{7,0},{8,15},{9,14},{10,... | collective-permute-start | bytes 294920 | tf_op jit(solution)/shard_map/ppermute | solution.py:387
  130.7 2.4 %collective-permute-start.43 = (bf16[48,1024]{1,0:T(8,128)(2,1)S(1)}, bf16[48,1024]{1,0:T(8,128)(2,1)S(1)}, u32[]{:S(2)}, u32[]{:S(2)}) collective-permute-start(bf16[48,1024]{1,0:T(8,128)(2,1)S(1)} %get-tuple-element.155), channel_id=1, source_target_pairs={{0,4},{1,5},{2,6},{3,7},{4,0},{5,1},{6,2},{7,3},{8,12},{9,13},{10,... | collective-permute-start | bytes 294920 | tf_op jit(solution)/shard_map/ppermute | solution.py:387
  133.4 1.7 collective-permute-start.44
  138.1 1.7 collective-permute-start.47
  141.2 3.6 %orthogonal.1 = (bf16[384,1024]{1,0:T(8,128)(2,1)}, bf16[384,1024]{1,0:T(8,128)(2,1)S(1)}) custom-call(s32[1]{0:T(128)} %bitcast.me_ref, f32[384,1024]{1,0:T(8,128)S(1)} %get-tuple-element.119.grad_ref, bf16[48,1024]{1,0:T(8,128)(2,1)S(1)} %get-tuple-element.131.refs_0_, bf16[48,1024]{1,0:T(8,128)(2,1)S(1)} %collective-permute-done.28.refs_1_, ...), custom_call_target="tpu_custom_call" | custom-call | flops 1434451968 | bytes 3932160 | tf_op jit(solution)/shard_map/orthogonal/pallas_call | solution.py:292
  144.9 2.4 %collective-permute-done.48.refs_6_ = bf16[48,1024]{1,0:T(8,128)(2,1)S(1)} collective-permute-done((bf16[48,1024]{1,0:T(8,128)(2,1)S(1)}, bf16[48,1024]{1,0:T(8,128)(2,1)S(1)}, u32[]{:S(2)}, u32[]{:S(2)}) %collective-permute-start.48) | collective-permute-done | bytes 98336 | tf_op jit(solution)/shard_map/ppermute | solution.py:387
  149.4 1.8 %collective-permute-start.51 = (bf16[32,1024]{1,0:T(8,128)(2,1)S(1)}, bf16[32,1024]{1,0:T(8,128)(2,1)S(1)}, u32[]{:S(2)}, u32[]{:S(2)}) collective-permute-start(bf16[32,1024]{1,0:T(8,128)(2,1)S(1)} %get-tuple-element.167), channel_id=1, source_target_pairs={{0,9},{1,8},{2,11},{3,10},{4,13},{5,12},{6,15},{7,14},{8,1},{9,0},... | collective-permute-start | bytes 196616 | tf_op jit(solution)/shard_map/ppermute | solution.py:387
  151.3 1.9 %collective-permute-start.52 = (bf16[32,1024]{1,0:T(8,128)(2,1)S(1)}, bf16[32,1024]{1,0:T(8,128)(2,1)S(1)}, u32[]{:S(2)}, u32[]{:S(2)}) collective-permute-start(bf16[32,1024]{1,0:T(8,128)(2,1)S(1)} %get-tuple-element.168), channel_id=1, source_target_pairs={{0,7},{1,6},{2,5},{3,4},{4,3},{5,2},{6,1},{7,0},{8,15},{9,14},{10,... | collective-permute-start | bytes 196616 | tf_op jit(solution)/shard_map/ppermute | solution.py:387
  154.5 1.7 collective-permute-start.54
  157.6 2.0 %collective-permute-start.56 = (bf16[32,1024]{1,0:T(8,128)(2,1)S(1)}, bf16[32,1024]{1,0:T(8,128)(2,1)S(1)}, u32[]{:S(2)}, u32[]{:S(2)}) collective-permute-start(bf16[32,1024]{1,0:T(8,128)(2,1)S(1)} %get-tuple-element.172), channel_id=1, source_target_pairs={{0,12},{1,13},{2,14},{3,15},{4,8},{5,9},{6,10},{7,11},{8,4},{9,5},... | collective-permute-start | bytes 196616 | tf_op jit(solution)/shard_map/ppermute | solution.py:387
  159.6 5.1 %collective-permute-start.57 = (bf16[32,1024]{1,0:T(8,128)(2,1)S(1)}, bf16[32,1024]{1,0:T(8,128)(2,1)S(1)}, u32[]{:S(2)}, u32[]{:S(2)}) collective-permute-start(bf16[32,1024]{1,0:T(8,128)(2,1)S(1)} %get-tuple-element.173), channel_id=1, source_target_pairs={{0,13},{1,12},{2,15},{3,14},{4,9},{5,8},{6,11},{7,10},{8,5},{9,4},... | collective-permute-start | bytes 196616 | tf_op jit(solution)/shard_map/ppermute | solution.py:387
  166.0 3.5 %collective-permute-start.60 = (bf16[32,1024]{1,0:T(8,128)(2,1)S(1)}, bf16[32,1024]{1,0:T(8,128)(2,1)S(1)}, u32[]{:S(2)}, u32[]{:S(2)}) collective-permute-start(bf16[32,1024]{1,0:T(8,128)(2,1)S(1)} %get-tuple-element.176), channel_id=1, source_target_pairs={{0,15},{1,14},{2,13},{3,12},{4,11},{5,10},{6,9},{7,8},{8,7},{9,6},... | collective-permute-start | bytes 196616 | tf_op jit(solution)/shard_map/ppermute | solution.py:387
  (160 shorter events, 59.7 us)
Async XLA Ops:
  3.5 11.3 %collective-permute-start.19 = (bf16[48,1024]{1,0:T(8,128)(2,1)}, bf16[48,1024]{1,0:T(8,128)(2,1)S(1)}, u32[]{:S(2)}, u32[]{:S(2)}) collective-permute-start(bf16[48,1024]{1,0:T(8,128)(2,1)} %get-tuple-element.120), channel_id=1, source_target_pairs={{0,4},{1,5},{2,6},{3,7},{4,0},{5,1},{6,2},{7,3},{8,12},{9,13},{10,... | collective-permute-start | bytes 294920 | tf_op jit(solution)/shard_map/ppermute | solution.py:387
  6.5 9.8 %collective-permute-start.20 = (bf16[48,1024]{1,0:T(8,128)(2,1)}, bf16[48,1024]{1,0:T(8,128)(2,1)S(1)}, u32[]{:S(2)}, u32[]{:S(2)}) collective-permute-start(bf16[48,1024]{1,0:T(8,128)(2,1)} %get-tuple-element.121), channel_id=1, source_target_pairs={{0,5},{1,4},{2,7},{3,6},{4,1},{5,0},{6,3},{7,2},{8,13},{9,12},{10,... | collective-permute-start | bytes 294920 | tf_op jit(solution)/shard_map/ppermute | solution.py:387
  6.5 30.2 %collective-permute-start.21 = (bf16[48,1024]{1,0:T(8,128)(2,1)}, bf16[48,1024]{1,0:T(8,128)(2,1)S(1)}, u32[]{:S(2)}, u32[]{:S(2)}) collective-permute-start(bf16[48,1024]{1,0:T(8,128)(2,1)} %get-tuple-element.122), channel_id=1, source_target_pairs={{0,3},{1,2},{2,1},{3,0},{4,7},{5,6},{6,5},{7,4},{8,11},{9,10},{10,... | collective-permute-start | bytes 294920 | tf_op jit(solution)/shard_map/ppermute | solution.py:387
  8.2 30.3 %collective-permute-start.22 = (bf16[48,1024]{1,0:T(8,128)(2,1)}, bf16[48,1024]{1,0:T(8,128)(2,1)S(1)}, u32[]{:S(2)}, u32[]{:S(2)}) collective-permute-start(bf16[48,1024]{1,0:T(8,128)(2,1)} %get-tuple-element.123), channel_id=1, source_target_pairs={{0,6},{1,7},{2,4},{3,5},{4,2},{5,3},{6,0},{7,1},{8,14},{9,15},{10,... | collective-permute-start | bytes 294920 | tf_op jit(solution)/shard_map/ppermute | solution.py:387
  14.8 23.8 %collective-permute-start.23 = (bf16[48,1024]{1,0:T(8,128)(2,1)}, bf16[48,1024]{1,0:T(8,128)(2,1)S(1)}, u32[]{:S(2)}, u32[]{:S(2)}) collective-permute-start(bf16[48,1024]{1,0:T(8,128)(2,1)} %get-tuple-element.124), channel_id=1, source_target_pairs={{0,7},{1,6},{2,5},{3,4},{4,3},{5,2},{6,1},{7,0},{8,15},{9,14},{10,... | collective-permute-start | bytes 294920 | tf_op jit(solution)/shard_map/ppermute | solution.py:387
  14.8 25.5 %collective-permute-start.24 = (bf16[48,1024]{1,0:T(8,128)(2,1)}, bf16[48,1024]{1,0:T(8,128)(2,1)S(1)}, u32[]{:S(2)}, u32[]{:S(2)}) collective-permute-start(bf16[48,1024]{1,0:T(8,128)(2,1)} %get-tuple-element.125), channel_id=1, source_target_pairs={{0,2},{1,3},{2,0},{3,1},{4,6},{5,7},{6,4},{7,5},{8,10},{9,11},{10,... | collective-permute-start | bytes 294920 | tf_op jit(solution)/shard_map/ppermute | solution.py:387
  16.3 26.7 %collective-permute-start.25 = (bf16[48,1024]{1,0:T(8,128)(2,1)}, bf16[48,1024]{1,0:T(8,128)(2,1)S(1)}, u32[]{:S(2)}, u32[]{:S(2)}) collective-permute-start(bf16[48,1024]{1,0:T(8,128)(2,1)} %get-tuple-element.126), channel_id=1, source_target_pairs={{0,1},{1,0},{2,3},{3,2},{4,5},{5,4},{6,7},{7,6},{8,9},{9,8},{10,11... | collective-permute-start | bytes 294920 | tf_op jit(solution)/shard_map/ppermute | solution.py:387
  36.7 8.8 %collective-permute-start.35 = (bf16[48,1024]{1,0:T(8,128)(2,1)}, bf16[48,1024]{1,0:T(8,128)(2,1)S(1)}, u32[]{:S(2)}, u32[]{:S(2)}) collective-permute-start(bf16[48,1024]{1,0:T(8,128)(2,1)} %get-tuple-element.143), channel_id=1, source_target_pairs={{0,4},{1,5},{2,6},{3,7},{4,0},{5,1},{6,2},{7,3},{8,12},{9,13},{10,... | collective-permute-start | bytes 294920 | tf_op jit(solution)/shard_map/ppermute | solution.py:387
  40.2 8.9 %collective-permute-start.38 = (bf16[48,1024]{1,0:T(8,128)(2,1)}, bf16[48,1024]{1,0:T(8,128)(2,1)S(1)}, u32[]{:S(2)}, u32[]{:S(2)}) collective-permute-start(bf16[48,1024]{1,0:T(8,128)(2,1)} %get-tuple-element.146), channel_id=1, source_target_pairs={{0,6},{1,7},{2,4},{3,5},{4,2},{5,3},{6,0},{7,1},{8,14},{9,15},{10,... | collective-permute-start | bytes 294920 | tf_op jit(solution)/shard_map/ppermute | solution.py:387
  46.4 15.8 %collective-permute-start.4 = (bf16[32,1792]{1,0:T(8,128)(2,1)}, bf16[32,1792]{1,0:T(8,128)(2,1)S(1)}, u32[]{:S(2)}, u32[]{:S(2)}) collective-permute-start(bf16[32,1792]{1,0:T(8,128)(2,1)} %get-tuple-element.104), channel_id=1, source_target_pairs={{0,8},{1,9},{2,10},{3,11},{4,12},{5,13},{6,14},{7,15},{8,0},{9,1},... | collective-permute-start | bytes 344072 | tf_op jit(solution)/shard_map/ppermute | solution.py:387
  49.1 13.1 %collective-permute-start.5 = (bf16[32,1792]{1,0:T(8,128)(2,1)}, bf16[32,1792]{1,0:T(8,128)(2,1)S(1)}, u32[]{:S(2)}, u32[]{:S(2)}) collective-permute-start(bf16[32,1792]{1,0:T(8,128)(2,1)} %get-tuple-element.105), channel_id=1, source_target_pairs={{0,7},{1,6},{2,5},{3,4},{4,3},{5,2},{6,1},{7,0},{8,15},{9,14},{10,... | collective-permute-start | bytes 344072 | tf_op jit(solution)/shard_map/ppermute | solution.py:387
  51.1 14.1 %collective-permute-start.6 = (bf16[32,1792]{1,0:T(8,128)(2,1)}, bf16[32,1792]{1,0:T(8,128)(2,1)S(1)}, u32[]{:S(2)}, u32[]{:S(2)}) collective-permute-start(bf16[32,1792]{1,0:T(8,128)(2,1)} %get-tuple-element.106), channel_id=1, source_target_pairs={{0,9},{1,8},{2,11},{3,10},{4,13},{5,12},{6,15},{7,14},{8,1},{9,0},... | collective-permute-start | bytes 344072 | tf_op jit(solution)/shard_map/ppermute | solution.py:387
  53.0 12.1 %collective-permute-start.7 = (bf16[32,1792]{1,0:T(8,128)(2,1)}, bf16[32,1792]{1,0:T(8,128)(2,1)S(1)}, u32[]{:S(2)}, u32[]{:S(2)}) collective-permute-start(bf16[32,1792]{1,0:T(8,128)(2,1)} %get-tuple-element.107), channel_id=1, source_target_pairs={{0,6},{1,7},{2,4},{3,5},{4,2},{5,3},{6,0},{7,1},{8,14},{9,15},{10,... | collective-permute-start | bytes 344072 | tf_op jit(solution)/shard_map/ppermute | solution.py:387
  57.2 28.4 %collective-permute-start.8 = (bf16[32,1792]{1,0:T(8,128)(2,1)}, bf16[32,1792]{1,0:T(8,128)(2,1)S(1)}, u32[]{:S(2)}, u32[]{:S(2)}) collective-permute-start(bf16[32,1792]{1,0:T(8,128)(2,1)} %copy-done.20), channel_id=1, source_target_pairs={{0,10},{1,11},{2,8},{3,9},{4,14},{5,15},{6,12},{7,13},{8,2},{9,3},... | collective-permute-start | bytes 344072 | tf_op jit(solution)/shard_map/ppermute | solution.py:387
  62.2 56.3 %collective-permute-start.26 = (bf16[4,48,1024]{2,1,0:T(8,128)(2,1)S(1)}, bf16[4,48,1024]{2,1,0:T(8,128)(2,1)S(1)}, u32[]{:S(2)}, u32[]{:S(2)}) collective-permute-start(bf16[4,48,1024]{2,1,0:T(8,128)(2,1)S(1)} %get-tuple-element.128), channel_id=1, source_target_pairs={{0,8},{1,9},{2,10},{3,11},{4,12},{5,13},{6,14},{7,15},{8,0},{9,1},... | collective-permute-start | bytes 1179656 | tf_op jit(solution)/shard_map/ppermute | solution.py:387
  62.2 63.1 %collective-permute-start.42 = (bf16[4,48,1024]{2,1,0:T(8,128)(2,1)S(1)}, bf16[4,48,1024]{2,1,0:T(8,128)(2,1)S(1)}, u32[]{:S(2)}, u32[]{:S(2)}) collective-permute-start(bf16[4,48,1024]{2,1,0:T(8,128)(2,1)S(1)} %get-tuple-element.151), channel_id=1, source_target_pairs={{0,8},{1,9},{2,10},{3,11},{4,12},{5,13},{6,14},{7,15},{8,0},{9,1},... | collective-permute-start | bytes 1179656 | tf_op jit(solution)/shard_map/ppermute | solution.py:387
  65.1 20.4 %collective-permute-start.9 = (bf16[32,1792]{1,0:T(8,128)(2,1)}, bf16[32,1792]{1,0:T(8,128)(2,1)S(1)}, u32[]{:S(2)}, u32[]{:S(2)}) collective-permute-start(bf16[32,1792]{1,0:T(8,128)(2,1)} %copy-done.19), channel_id=1, source_target_pairs={{0,5},{1,4},{2,7},{3,6},{4,1},{5,0},{6,3},{7,2},{8,13},{9,12},{10,... | collective-permute-start | bytes 344072 | tf_op jit(solution)/shard_map/ppermute | solution.py:387
  65.1 43.9 %collective-permute-start.10 = (bf16[32,1792]{1,0:T(8,128)(2,1)}, bf16[32,1792]{1,0:T(8,128)(2,1)S(1)}, u32[]{:S(2)}, u32[]{:S(2)}) collective-permute-start(bf16[32,1792]{1,0:T(8,128)(2,1)} %copy-done.18), channel_id=1, source_target_pairs={{0,11},{1,10},{2,9},{3,8},{4,15},{5,14},{6,13},{7,12},{8,3},{9,2},... | collective-permute-start | bytes 344072 | tf_op jit(solution)/shard_map/ppermute | solution.py:387
  85.5 25.6 %collective-permute-start.11 = (bf16[32,1792]{1,0:T(8,128)(2,1)}, bf16[32,1792]{1,0:T(8,128)(2,1)S(1)}, u32[]{:S(2)}, u32[]{:S(2)}) collective-permute-start(bf16[32,1792]{1,0:T(8,128)(2,1)} %copy-done.17), channel_id=1, source_target_pairs={{0,4},{1,5},{2,6},{3,7},{4,0},{5,1},{6,2},{7,3},{8,12},{9,13},{10,... | collective-permute-start | bytes 344072 | tf_op jit(solution)/shard_map/ppermute | solution.py:387
  85.5 26.3 %collective-permute-start.12 = (bf16[32,1792]{1,0:T(8,128)(2,1)}, bf16[32,1792]{1,0:T(8,128)(2,1)S(1)}, u32[]{:S(2)}, u32[]{:S(2)}) collective-permute-start(bf16[32,1792]{1,0:T(8,128)(2,1)} %copy-done.16), channel_id=1, source_target_pairs={{0,12},{1,13},{2,14},{3,15},{4,8},{5,9},{6,10},{7,11},{8,4},{9,5},... | collective-permute-start | bytes 344072 | tf_op jit(solution)/shard_map/ppermute | solution.py:387
  111.8 10.2 %collective-permute-start.15 = (bf16[32,1792]{1,0:T(8,128)(2,1)}, bf16[32,1792]{1,0:T(8,128)(2,1)S(1)}, u32[]{:S(2)}, u32[]{:S(2)}) collective-permute-start(bf16[32,1792]{1,0:T(8,128)(2,1)} %copy-done.13), channel_id=1, source_target_pairs={{0,2},{1,3},{2,0},{3,1},{4,6},{5,7},{6,4},{7,5},{8,10},{9,11},{10,... | collective-permute-start | bytes 344072 | tf_op jit(solution)/shard_map/ppermute | solution.py:387
  118.5 8.5 %collective-permute-start.18 = (bf16[32,1792]{1,0:T(8,128)(2,1)}, bf16[32,1792]{1,0:T(8,128)(2,1)S(1)}, u32[]{:S(2)}, u32[]{:S(2)}) collective-permute-start(bf16[32,1792]{1,0:T(8,128)(2,1)} %copy-done.10), channel_id=1, source_target_pairs={{0,15},{1,14},{2,13},{3,12},{4,11},{5,10},{6,9},{7,8},{8,7},{9,6},... | collective-permute-start | bytes 344072 | tf_op jit(solution)/shard_map/ppermute | solution.py:387
  127.0 8.7 %collective-permute-start.32 = (bf16[48,1024]{1,0:T(8,128)(2,1)S(1)}, bf16[48,1024]{1,0:T(8,128)(2,1)S(1)}, u32[]{:S(2)}, u32[]{:S(2)}) collective-permute-start(bf16[48,1024]{1,0:T(8,128)(2,1)S(1)} %get-tuple-element.136), channel_id=1, source_target_pairs={{0,7},{1,6},{2,5},{3,4},{4,3},{5,2},{6,1},{7,0},{8,15},{9,14},{10,... | collective-permute-start | bytes 294920 | tf_op jit(solution)/shard_map/ppermute | solution.py:387
  130.7 9.1 %collective-permute-start.43 = (bf16[48,1024]{1,0:T(8,128)(2,1)S(1)}, bf16[48,1024]{1,0:T(8,128)(2,1)S(1)}, u32[]{:S(2)}, u32[]{:S(2)}) collective-permute-start(bf16[48,1024]{1,0:T(8,128)(2,1)S(1)} %get-tuple-element.155), channel_id=1, source_target_pairs={{0,4},{1,5},{2,6},{3,7},{4,0},{5,1},{6,2},{7,3},{8,12},{9,13},{10,... | collective-permute-start | bytes 294920 | tf_op jit(solution)/shard_map/ppermute | solution.py:387
  135.8 9.1 %collective-permute-start.45 = (bf16[48,1024]{1,0:T(8,128)(2,1)S(1)}, bf16[48,1024]{1,0:T(8,128)(2,1)S(1)}, u32[]{:S(2)}, u32[]{:S(2)}) collective-permute-start(bf16[48,1024]{1,0:T(8,128)(2,1)S(1)} %get-tuple-element.157), channel_id=1, source_target_pairs={{0,3},{1,2},{2,1},{3,0},{4,7},{5,6},{6,5},{7,4},{8,11},{9,10},{10,... | collective-permute-start | bytes 294920 | tf_op jit(solution)/shard_map/ppermute | solution.py:387
  148.9 8.6 %collective-permute-start.50 = (bf16[32,1024]{1,0:T(8,128)(2,1)S(1)}, bf16[32,1024]{1,0:T(8,128)(2,1)S(1)}, u32[]{:S(2)}, u32[]{:S(2)}) collective-permute-start(bf16[32,1024]{1,0:T(8,128)(2,1)S(1)} %get-tuple-element.166), channel_id=1, source_target_pairs={{0,8},{1,9},{2,10},{3,11},{4,12},{5,13},{6,14},{7,15},{8,0},{9,1},... | collective-permute-start | bytes 196616 | tf_op jit(solution)/shard_map/ppermute | solution.py:387
  151.3 8.3 %collective-permute-start.52 = (bf16[32,1024]{1,0:T(8,128)(2,1)S(1)}, bf16[32,1024]{1,0:T(8,128)(2,1)S(1)}, u32[]{:S(2)}, u32[]{:S(2)}) collective-permute-start(bf16[32,1024]{1,0:T(8,128)(2,1)S(1)} %get-tuple-element.168), channel_id=1, source_target_pairs={{0,7},{1,6},{2,5},{3,4},{4,3},{5,2},{6,1},{7,0},{8,15},{9,14},{10,... | collective-permute-start | bytes 196616 | tf_op jit(solution)/shard_map/ppermute | solution.py:387
  153.2 11.5 %collective-permute-start.53 = (bf16[32,1024]{1,0:T(8,128)(2,1)S(1)}, bf16[32,1024]{1,0:T(8,128)(2,1)S(1)}, u32[]{:S(2)}, u32[]{:S(2)}) collective-permute-start(bf16[32,1024]{1,0:T(8,128)(2,1)S(1)} %get-tuple-element.169), channel_id=1, source_target_pairs={{0,10},{1,11},{2,8},{3,9},{4,14},{5,15},{6,12},{7,13},{8,2},{9,3},... | collective-permute-start | bytes 196616 | tf_op jit(solution)/shard_map/ppermute | solution.py:387
  154.5 10.2 %collective-permute-start.54 = (bf16[32,1024]{1,0:T(8,128)(2,1)S(1)}, bf16[32,1024]{1,0:T(8,128)(2,1)S(1)}, u32[]{:S(2)}, u32[]{:S(2)}) collective-permute-start(bf16[32,1024]{1,0:T(8,128)(2,1)S(1)} %get-tuple-element.170), channel_id=1, source_target_pairs={{0,11},{1,10},{2,9},{3,8},{4,15},{5,14},{6,13},{7,12},{8,3},{9,2},... | collective-permute-start | bytes 196616 | tf_op jit(solution)/shard_map/ppermute | solution.py:387
  157.6 8.4 %collective-permute-start.55 = (bf16[32,1024]{1,0:T(8,128)(2,1)S(1)}, bf16[32,1024]{1,0:T(8,128)(2,1)S(1)}, u32[]{:S(2)}, u32[]{:S(2)}) collective-permute-start(bf16[32,1024]{1,0:T(8,128)(2,1)S(1)} %get-tuple-element.171), channel_id=1, source_target_pairs={{0,6},{1,7},{2,4},{3,5},{4,2},{5,3},{6,0},{7,1},{8,14},{9,15},{10,... | collective-permute-start | bytes 196616 | tf_op jit(solution)/shard_map/ppermute | solution.py:387
  157.6 12.0 %collective-permute-start.56 = (bf16[32,1024]{1,0:T(8,128)(2,1)S(1)}, bf16[32,1024]{1,0:T(8,128)(2,1)S(1)}, u32[]{:S(2)}, u32[]{:S(2)}) collective-permute-start(bf16[32,1024]{1,0:T(8,128)(2,1)S(1)} %get-tuple-element.172), channel_id=1, source_target_pairs={{0,12},{1,13},{2,14},{3,15},{4,8},{5,9},{6,10},{7,11},{8,4},{9,5},... | collective-permute-start | bytes 196616 | tf_op jit(solution)/shard_map/ppermute | solution.py:387
  159.6 9.9 %collective-permute-start.57 = (bf16[32,1024]{1,0:T(8,128)(2,1)S(1)}, bf16[32,1024]{1,0:T(8,128)(2,1)S(1)}, u32[]{:S(2)}, u32[]{:S(2)}) collective-permute-start(bf16[32,1024]{1,0:T(8,128)(2,1)S(1)} %get-tuple-element.173), channel_id=1, source_target_pairs={{0,13},{1,12},{2,15},{3,14},{4,9},{5,8},{6,11},{7,10},{8,5},{9,4},... | collective-permute-start | bytes 196616 | tf_op jit(solution)/shard_map/ppermute | solution.py:387
  (56 other events, 449.3 us)
where the time goes:
time: 178 us
  starting transfers between devices  77.8 us (44%)
  waiting for transfers between devices  59.3 us (33%)
  Pallas kernels  21.5 us (12%)
  local copies, waits for them, and re-layouts  15 us (8%)
  between operations  2.82 us (2%)
    ppermute x60, starting transfers between devices, swap(): lax.ppermute(piece, 'expert', [(i, i ^ s) for i in range(groups)])  76.3 us
    ppermute x60, waiting for transfers between devices, swap(): lax.ppermute(piece, 'expert', [(i, i ^ s) for i in range(groups)])  57.1 us
    unnamed x54, local copies, waits for them, and re-layouts  15 us
    pallas_call x2, Pallas kernels, split(): pl.pallas_call(split_kernel, out_shape=(piece,) * half, in_specs=[SMEM, H...  4.93 us
    pallas_call x1, Pallas kernels, orthogonal(): pl.pallas_call(orthogonal_kernel, out_shape=(shape, shape), in_specs=[SME...  3.65 us
  transfers between devices with their start and end apart: 61, of which 18 were waited for; matrix products, arithmetic and copies ran while one was open for 1% of the time, Pallas kernels for 9%

commit v1 on v0

--- a/solution.py
+++ b/solution.py
@@ -61,88 +61,91 @@
     return jnp.where(places == slot, 1.0, 0.0).astype(BF16)
 
 
-def pack_kernel(groups, live_ref, me_ref, perm_ref, *refs):
-    sources, pieces, (slot_ref, gates_ref) = refs[:6], refs[7 : 7 + groups], refs[7 + groups : 9 + groups]
-    held, sem = refs[9 + groups : 15 + groups], refs[-1]
-    route_ref, fwd_route_ref, hidden_ref, out_ref, fwd_ref, gate_ref = held
-    copies = [pltpu.make_async_copy(ref, room, sem.at[n]) for n, (ref, room) in enumerate(zip(sources, held))]
+def prepare_kernel(groups, half, live_ref, me_ref, perm_ref, *refs):
+    sources, refs = refs[:8], refs[8:]
+    moment_pieces, weight_pieces, packed_pieces = refs[:half], refs[half : 2 * half], refs[2 * half : 2 * half + groups]
+    slot_ref, gates_ref = refs[2 * half + groups : 2 * half + groups + 2]
+    *held, packed, in_sem, out_sem = refs[2 * half + groups + 2 :]
+    moment_ref, route_ref, fwd_route_ref, hidden_ref, out_ref, fwd_ref, gate_ref, weight_ref = held
+    copies = [pltpu.make_async_copy(ref, room, in_sem.at[n]) for n, (ref, room) in enumerate(zip(sources, held))]
     for copy in copies:
         copy.start()
     rows, ff = hidden_ref.shape
     d = out_ref.shape[1]
-    capacity = pieces[0].shape[0]
+    capacity = packed_pieces[0].shape[0]
     slots = groups * capacity
     place = lax.broadcasted_iota(jnp.int32, (1, rows), 1)
-
-    def fill(first, selector, source_ref):
-        chosen = jnp.dot(selector, source_ref[...], preferred_element_type=F32).astype(BF16)
-        for s, piece in zip(mixed_order(groups), pieces):
-            piece[:, first : first + source_ref.shape[1]] = chosen[s * capacity : (s + 1) * capacity]
+    leaving = []
+
+    def leave(source, piece):
+        copy = pltpu.make_async_copy(source, piece, out_sem.at[len(leaving)])
+        copy.start()
+        leaving.append(copy)
+
+    def leave_blocks(matrix, pieces):
+        for s, piece in zip(return_order(half), pieces):
+            leave(matrix.at[0, row_block((me_ref[0] ^ s) % half, piece.shape[0])], piece)
 
     copies[0].wait()
+    leave_blocks(moment_ref, moment_pieces)
+    copies[1].wait()
     slot = slot_rows(route_ref[...], place < live_ref[0], groups, capacity, me_ref, perm_ref)
     selector = selector_of(slot, slots)
-    copies[1].wait()
+    copies[2].wait()
     fwd_slot = slot_rows(fwd_route_ref[...], place >= 0, groups, capacity, me_ref, perm_ref)
     slot_ref[...] = fwd_slot
-    copies[2].wait()
-    fill(0, selector, hidden_ref)
     copies[3].wait()
-    fill(ff, selector, out_ref)
+    packed[:, :ff] = jnp.dot(selector, hidden_ref[...], preferred_element_type=F32).astype(BF16)
     copies[4].wait()
-    fill(ff + d, selector_of(fwd_slot, slots), fwd_ref)
+    packed[:, ff : ff + d] = jnp.dot(selector, out_ref[...], preferred_element_type=F32).astype(BF16)
     copies[5].wait()
+    fwd_selector = selector_of(fwd_slot, slots)
+    packed[:, ff + d :] = jnp.dot(fwd_selector, fwd_ref[...], preferred_element_type=F32).astype(BF16)
+    for s, piece in zip(mixed_order(groups), packed_pieces):
+        leave(packed.at[pl.ds(s * capacity, capacity)], piece)
+    copies[7].wait()
+    leave_blocks(weight_ref, weight_pieces)
+    copies[6].wait()
     down = lax.broadcasted_iota(jnp.int32, (rows, rows), 0)
     across = lax.broadcasted_iota(jnp.int32, (rows, rows), 1)
     gates_ref[...] = jnp.sum(jnp.where(down == across, gate_ref[...], 0.0), axis=1, keepdims=True)
-
-
-def pack_rows(live_rows, me, perm, route, fwd_route, hidden, grad_out, fwd_hidden, gate, earlier, groups, capacity):
+    for copy in leaving:
+        copy.wait()
+
+
+def prepare(live_rows, me, perm, route, fwd_route, hidden, grad_out, fwd_hidden, gate, moment, weight, groups, capacity):
     rows, ff = hidden.shape
-    width = 2 * ff + grad_out.shape[1]
-    sources = (route.reshape(1, rows), fwd_route.reshape(1, rows), hidden, grad_out, fwd_hidden, gate.reshape(1, rows))
-    *pieces, slot, gates = pl.pallas_call(
-        functools.partial(pack_kernel, groups),
-        out_shape=(jax.ShapeDtypeStruct((capacity, width), BF16),) * groups
+    d = grad_out.shape[1]
+    half = groups // 2
+    width = 2 * ff + d
+    sources = (
+        moment, route.reshape(1, rows), fwd_route.reshape(1, rows), hidden, grad_out, fwd_hidden,
+        gate.reshape(1, rows), weight,
+    )
+    block = jax.ShapeDtypeStruct((ff // half, d), BF16)
+    outputs = pl.pallas_call(
+        functools.partial(prepare_kernel, groups, half),
+        out_shape=(block,) * (2 * half)
+        + (jax.ShapeDtypeStruct((capacity, width), BF16),) * groups
         + (jax.ShapeDtypeStruct((1, rows), jnp.int32), jax.ShapeDtypeStruct((rows, 1), F32)),
-        in_specs=[SMEM] * 3 + [HBM] * 6 + [VMEM],
-        out_specs=(VMEM,) * (groups + 2),
-        scratch_shapes=[pltpu.VMEM(a.shape, a.dtype) for a in sources] + [pltpu.SemaphoreType.DMA((len(sources),))],
-        compiler_params=pltpu.CompilerParams(vmem_limit_bytes=32 * MIB),
+        in_specs=[SMEM] * 3 + [HBM] * len(sources),
+        out_specs=(HBM,) * (2 * half + groups) + (VMEM, VMEM),
+        scratch_shapes=[pltpu.VMEM(a.shape, a.dtype) for a in sources]
+        + [
+            pltpu.VMEM((groups * capacity, width), BF16),
+            pltpu.SemaphoreType.DMA((len(sources),)),
+            pltpu.SemaphoreType.DMA((2 * half + groups,)),
+        ],
+        compiler_params=pltpu.CompilerParams(vmem_limit_bytes=60 * MIB),
         cost_estimate=pl.CostEstimate(
-            flops=2 * groups * capacity * rows * width, bytes_accessed=6 * rows * width, transcendentals=0
+            flops=2 * groups * capacity * rows * width,
+            bytes_accessed=8 * ff * d + 6 * rows * width,
+            transcendentals=0,
         ),
-        name="pack_rows",
-    )(live_rows, me, perm, *sources, earlier)
-    return pieces, slot, gates
-
-
-def split_kernel(me_ref, matrix_ref, *refs):
-    pieces, sem = refs[1:-1], refs[-1]
-    half, rows = len(pieces), pieces[0].shape[0]
-    copies = [
-        pltpu.make_async_copy(matrix_ref.at[0, row_block((me_ref[0] ^ s) % half, rows)], piece, sem.at[s])
-        for s, piece in zip(return_order(half), pieces)
-    ]
-    for copy in copies:
-        copy.start()
-    for copy in copies:
-        copy.wait()
-
-
-def split(me, matrix, earlier, half):
-    _, ff, d = matrix.shape
-    piece = jax.ShapeDtypeStruct((ff // half, d), BF16)
-    return pl.pallas_call(
-        split_kernel,
-        out_shape=(piece,) * half,
-        in_specs=[SMEM, HBM, VMEM],
-        out_specs=(VMEM,) * half,
-        scratch_shapes=[pltpu.SemaphoreType.DMA((half,))],
-        compiler_params=pltpu.CompilerParams(vmem_limit_bytes=60 * MIB),
-        cost_estimate=pl.CostEstimate(flops=0, bytes_accessed=4 * ff * d, transcendentals=0),
-        name="split",
-    )(me, matrix, earlier)
+        name="prepare",
+    )(live_rows, me, perm, *sources)
+    *pieces, slot, gates = outputs
+    return pieces[:half], pieces[half : 2 * half], pieces[2 * half :], slot, gates
 
 
 def sort_kernel(me_ref, perm_ref, *refs):
@@ -183,14 +186,14 @@
         out_shape=tuple(jax.ShapeDtypeStruct((count,) + shape, BF16) for count in counts),
         in_specs=[SMEM, SMEM] + [VMEM] * half,
         out_specs=(VMEM,) * len(counts),
-        compiler_params=pltpu.CompilerParams(vmem_limit_bytes=32 * MIB),
+        compiler_params=pltpu.CompilerParams(vmem_limit_bytes=60 * MIB),
         cost_estimate=pl.CostEstimate(flops=0, bytes_accessed=4 * half * pieces[0].size, transcendentals=0),
         name="sort_pieces",
     )(me, perm, *pieces)
 
 
 def join_kernel(half, me_ref, perm_ref, near_ref, *refs):
-    slot_refs, targets = refs[:3], refs[3:]
+    slot_refs, targets = refs[:3], refs[4:]
     me = me_ref[0]
     base = me // half * half
     flags, ranks = crossing_ranks(half, half - base, perm_ref)
@@ -216,48 +219,54 @@
             first += count
 
 
-def join_pieces(me, perm, near, slots):
+def join_pieces(me, perm, near, slots, earlier):
     half = near.shape[0]
     piece = jax.ShapeDtypeStruct(near.shape[1:], BF16)
     return pl.pallas_call(
         functools.partial(join_kernel, half),
         out_shape=(piece,) * half,
-        in_specs=[SMEM, SMEM] + [VMEM] * 4,
+        in_specs=[SMEM, SMEM] + [VMEM] * 5,
         out_specs=(VMEM,) * half,
-        compiler_params=pltpu.CompilerParams(vmem_limit_bytes=32 * MIB),
+        compiler_params=pltpu.CompilerParams(vmem_limit_bytes=60 * MIB),
         cost_estimate=pl.CostEstimate(flops=0, bytes_accessed=4 * near.size, transcendentals=0),
         name="join_pieces",
-    )(me, perm, near, *slots)
-
-
-def gradient_kernel(groups, *refs):
-    pieces, (grad_ref, fwd_ref, rows_ref) = refs[:groups], refs[groups:]
+    )(me, perm, near, *slots, earlier)
+
+
+def gradient_kernel(first, *refs):
+    count = len(refs) - 4 if first else len(refs) - 5
+    pieces, (grad_ref, fwd_ref, token_ref, rows_ref) = refs[:count], refs[-4:]
     ff, d = grad_ref.shape
     capacity = pieces[0].shape[0]
     for n, piece in enumerate(pieces):
         span = slice(n * capacity, (n + 1) * capacity)
         rows_ref[span] = piece[:, : ff + d]
         fwd_ref[span] = piece[:, ff + d :]
-    grad_ref[...] = lax.dot_general(
+    grad = lax.dot_general(
         rows_ref[:, :ff], rows_ref[:, ff:], (((0,), (0,)), ((), ())), preferred_element_type=F32
     )
-
-
-def gradient(pieces, ff, d):
-    groups = len(pieces)
-    slots = groups * pieces[0].shape[0]
+    grad_ref[...] = grad if first else refs[count][...] + grad
+    token_ref[...] = jnp.zeros_like(token_ref)
+
+
+def gradient(pieces, ff, d, *sofar):
+    slots = len(pieces) * pieces[0].shape[0]
     return pl.pallas_call(
-        functools.partial(gradient_kernel, groups),
-        out_shape=(jax.ShapeDtypeStruct((ff, d), F32), jax.ShapeDtypeStruct((slots, ff), BF16)),
-        in_specs=[VMEM] * groups,
-        out_specs=(VMEM, VMEM),
+        functools.partial(gradient_kernel, not sofar),
+        out_shape=(
+            jax.ShapeDtypeStruct((ff, d), F32),
+            jax.ShapeDtypeStruct((slots, ff), BF16),
+            jax.ShapeDtypeStruct((8, 128), F32),
+        ),
+        in_specs=[VMEM] * (len(pieces) + len(sofar)),
+        out_specs=(VMEM,) * 3,
         scratch_shapes=[pltpu.VMEM((slots, ff + d), BF16)],
         compiler_params=pltpu.CompilerParams(vmem_limit_bytes=32 * MIB),
         cost_estimate=pl.CostEstimate(
             flops=2 * ff * d * slots, bytes_accessed=4 * ff * d + 4 * slots * (ff + d), transcendentals=0
         ),
         name="gradient",
-    )(*pieces)
+    )(*pieces, *sofar)
 
 
 def assembled(me_ref, pieces, held):
@@ -303,28 +312,30 @@
     )(me, grad, *pieces)
 
 
-def produce_kernel(half, me_ref, ortho_ref, fwd_ref, *refs):
+def produce_kernel(half, me_ref, ortho_ref, early_ref, late_ref, *refs):
     pieces, (weight_new_ref, *produced), held = refs[:half], refs[half:-1], refs[-1]
     weight = assembled(me_ref, pieces, held)
     weight_new = (weight - step_scale * ortho_ref[...].astype(F32)).astype(BF16)
     weight_new_ref[...] = weight_new
-    product = jnp.dot(fwd_ref[...], weight_new, preferred_element_type=F32).astype(BF16)
+    products = [
+        jnp.dot(ref[...], weight_new, preferred_element_type=F32).astype(BF16) for ref in (early_ref, late_ref)
+    ]
     groups, capacity = len(produced), produced[0].shape[0]
     came = mixed_order(groups)
     for s, piece in zip(return_order(groups), produced):
-        n = came.index(s)
-        piece[...] = product[n * capacity : (n + 1) * capacity]
+        part, n = divmod(came.index(s), groups // 2)
+        piece[...] = products[part][n * capacity : (n + 1) * capacity]
 
 
 def produce(me, ortho, fwd_rows, pieces, groups):
     half = len(pieces)
     ff, d = ortho.shape
-    slots = fwd_rows.shape[0]
+    slots = 2 * fwd_rows[0].shape[0]
     weight_new, *produced = pl.pallas_call(
         functools.partial(produce_kernel, half),
         out_shape=(jax.ShapeDtypeStruct((ff, d), BF16),)
         + (jax.ShapeDtypeStruct((slots // groups, d), BF16),) * groups,
-        in_specs=[SMEM] + [VMEM] * (2 + half),
+        in_specs=[SMEM] + [VMEM] * (3 + half),
         out_specs=(VMEM,) * (groups + 1),
         scratch_shapes=[pltpu.VMEM((ff, d), BF16)],
         compiler_params=pltpu.CompilerParams(vmem_limit_bytes=32 * MIB),
@@ -332,7 +343,7 @@
             flops=2 * ff * d * slots, bytes_accessed=8 * ff * d + 2 * slots * (ff + d), transcendentals=0
         ),
         name="produce",
-    )(me, ortho, fwd_rows, *pieces)
+    )(me, ortho, *fwd_rows, *pieces)
     return weight_new, produced
 
 
@@ -410,27 +421,26 @@
     def mirror(array):
         return swap([array], [half])[0]
 
-    def gathered(spread):
+    def gathered(spread, earlier):
         near, first, following, rest = sort_pieces(me, perm, spread)
         crossed = [
             mirror(first),
             lax.cond(most > slot_counts[0], mirror, lambda array: array, following),
             lax.cond(most > slot_counts[0] + slot_counts[1], mirror, lambda array: array, rest),
         ]
-        return swap(join_pieces(me, perm, near, crossed), near_order)
-
-    moment_pieces = split(me, w_moment, live_rows, half)
-    packed, fwd_slot, gates = pack_rows(
-        live_rows, me, perm, grad_route, fwd_route, grad_hidden, grad_out, fwd_hidden, fwd_gate,
-        moment_pieces[0], groups, capacity,
-    )
-    weight_pieces = split(me, w_down, fwd_slot, half)
+        return swap(join_pieces(me, perm, near, crossed, earlier), near_order)
+
+    moment_pieces, weight_pieces, packed, fwd_slot, gates = prepare(
+        live_rows, me, perm, grad_route, fwd_route, grad_hidden, grad_out, fwd_hidden, fwd_gate, w_moment, w_down,
+        groups, capacity,
+    )
     received = swap(packed, mixed_order(groups))
-    moment_placed = gathered(swap(moment_pieces, near_order))
-    weight_placed = gathered(swap(weight_pieces, near_order))
-    grad, fwd_rows = gradient(received, ff, d)
+    early_grad, early_rows, token = gradient(received[:half], ff, d)
+    moment_placed = gathered(swap(moment_pieces, near_order), token)
+    weight_placed = gathered(swap(weight_pieces, near_order), token)
+    grad, late_rows, _ = gradient(received[half:], ff, d, early_grad)
     moment_new, ortho = orthogonal(me, grad, moment_placed)
-    weight_new, produced = produce(me, ortho, fwd_rows, weight_placed, groups)
+    weight_new, produced = produce(me, ortho, (early_rows, late_rows), weight_placed, groups)
     returned = swap(produced, return_order(groups))
     return weight_new[None], moment_new[None], finish(fwd_slot, gates, returned)
 

time: 178 us -> 170 us (0.955)
  local copies, waits for them, and re-layouts: 15 us -> 1.89 us
  waiting for transfers between devices: 59.3 us -> 69.3 us
  starting transfers between devices: 77.8 us -> 70 us
  Pallas kernels: 21.5 us -> 24.3 us
    unnamed x54 -> x84, local copies, waits for them, and re-layouts: 15 us -> 1.89 us
    ppermute x60, waiting for transfers between devices: 57.1 us -> 67.1 us  [swap(): lax.ppermute(piece, 'expert', [(i, i ^ s) for i in range(groups)])]
    ppermute x60, starting transfers between devices: 76.3 us -> 68.5 us  [swap(): lax.ppermute(piece, 'expert', [(i, i ^ s) for i in range(groups)])]
    pallas_call x2, Pallas kernels: 2.55 us -> 5.38 us  [join_pieces(): pl.pallas_call(functools.partial(join_kernel, half), out_shape=(piece,) *...]
    pallas_call x2, Pallas kernels: 3.43 us -> 5.43 us  [sort_pieces(): pl.pallas_call(sort_kernel, out_shape=tuple((jax.ShapeDtypeStruct((count,...]
    pallas_call x4 -> x3, Pallas kernels: 9.02 us -> 7.14 us  [the longest x1 5.78 us: prepare(): pl.pallas_call(functools.partial(prepare_kernel, groups, half), out_shape...]
  transfers between devices with their start and end apart: 61 -> 61, of which waited for: 18 -> 25; matrix products, arithmetic and copies ran while one was open for 1% -> 0% of each run, Pallas kernels for 9% -> 9%
where the time goes in v1:
time: 170 us; the launch traced here: 169 us
  starting transfers between devices  70 us (41%)
  waiting for transfers between devices  69.3 us (41%)
  Pallas kernels  24.3 us (14%)
  between operations  3.08 us (2%)
  local copies, waits for them, and re-layouts  1.89 us (1%)
    ppermute x60, starting transfers between devices, swap(): lax.ppermute(piece, 'expert', [(i, i ^ s) for i in range(groups)])  68.5 us
    ppermute x60, waiting for transfers between devices, swap(): lax.ppermute(piece, 'expert', [(i, i ^ s) for i in range(groups)])  67.1 us
    pallas_call x1, Pallas kernels, prepare(): pl.pallas_call(functools.partial(prepare_kernel, groups, half), out_shape...  5.78 us
    pallas_call x2, Pallas kernels, sort_pieces(): pl.pallas_call(sort_kernel, out_shape=tuple((jax.ShapeDtypeStruct((count,...  5.43 us
    pallas_call x2, Pallas kernels, join_pieces(): pl.pallas_call(functools.partial(join_kernel, half), out_shape=(piece,) *...  5.38 us
    pallas_call x1, Pallas kernels, orthogonal(): pl.pallas_call(orthogonal_kernel, out_shape=(shape, shape), in_specs=[SME...  3.61 us
  transfers between devices with their start and end apart: 61, of which 25 were waited for; matrix products, arithmetic and copies ran while one was open for 0% of the time, Pallas kernels for 9%

profile of v1, /device:TPU:0, one launch (start us, length us, event | category | flops | bytes accessed | tf_op | source)
XLA Modules:
  0.0 169.3 jit_solution(15268188238978775815)
XLA Ops:
  1.3 5.8 %prepare.1 = (bf16[48,1024]{1,0:T(8,128)(2,1)}, bf16[48,1024]{1,0:T(8,128)(2,1)}, bf16[48,1024]{1,0:T(8,128)(2,1)}, bf16[48,1024]{1,0:T(8,128)(2,1)}, bf16[48,10...) custom-call(s32[1]{0:T(128)S(6)} %copy.21.live_ref, ...), custom_call_target="tpu_custom_call" | custom-call | flops 469762048 | bytes 5898240 | tf_op jit(solution)/shard_map/prepare/pallas_call | solution.py:126
  7.1 3.1 %collective-permute-start.35 = (bf16[48,1024]{1,0:T(8,128)(2,1)}, bf16[48,1024]{1,0:T(8,128)(2,1)S(1)}, u32[]{:S(2)}, u32[]{:S(2)}) collective-permute-start(bf16[48,1024]{1,0:T(8,128)(2,1)} %get-tuple-element.148), channel_id=1, source_target_pairs={{0,4},{1,5},{2,6},{3,7},{4,0},{5,1},{6,2},{7,3},{8,12},{9,13},{10,... | collective-permute-start | bytes 294920 | tf_op jit(solution)/shard_map/ppermute | solution.py:398
  10.2 1.7 collective-permute-start.37
  15.5 2.2 %collective-permute-done.27 = s32[1]{0:T(128)} collective-permute-done((s32[1]{0:T(128)}, s32[1]{0:T(128)}, u32[]{:S(2)}, u32[]{:S(2)}) %collective-permute-start.27) | collective-permute-done | bytes 36 | tf_op jit(solution)/shard_map/ppermute | solution.py:415
  19.4 1.7 %collective-permute-start.19 = (bf16[48,1024]{1,0:T(8,128)(2,1)}, bf16[48,1024]{1,0:T(8,128)(2,1)S(1)}, u32[]{:S(2)}, u32[]{:S(2)}) collective-permute-start(bf16[48,1024]{1,0:T(8,128)(2,1)} %get-tuple-element.124), channel_id=1, source_target_pairs={{0,4},{1,5},{2,6},{3,7},{4,0},{5,1},{6,2},{7,3},{8,12},{9,13},{10,... | collective-permute-start | bytes 294920 | tf_op jit(solution)/shard_map/ppermute | solution.py:398
  21.2 1.9 %collective-permute-done.39.refs_5_ = bf16[48,1024]{1,0:T(8,128)(2,1)S(1)} collective-permute-done((bf16[48,1024]{1,0:T(8,128)(2,1)}, bf16[48,1024]{1,0:T(8,128)(2,1)S(1)}, u32[]{:S(2)}, u32[]{:S(2)}) %collective-permute-start.39) | collective-permute-done | bytes 98336 | tf_op jit(solution)/shard_map/ppermute | solution.py:398
  23.1 2.0 %collective-permute-done.40.refs_6_ = bf16[48,1024]{1,0:T(8,128)(2,1)S(1)} collective-permute-done((bf16[48,1024]{1,0:T(8,128)(2,1)}, bf16[48,1024]{1,0:T(8,128)(2,1)S(1)}, u32[]{:S(2)}, u32[]{:S(2)}) %collective-permute-start.40) | collective-permute-done | bytes 98336 | tf_op jit(solution)/shard_map/ppermute | solution.py:398
  28.6 2.8 %sort_pieces.3 = (bf16[8,48,1024]{2,1,0:T(8,128)(2,1)}, bf16[4,48,1024]{2,1,0:T(8,128)(2,1)}, bf16[1,48,1024]{2,1,0:T(8,128)(2,1)S(1)}, bf16[3,48,1024]{2,1,0:T(8,128)(2,1)S(1)}) custom-call(s32[1]{0:T(128)} %bitcast.me_ref, s32[16]{0:T(128)} %perm_ref.9, bf16[48,1024]{1,0:T(8,128)(2,1)} %get-tuple-element.147.refs_0_, bf16[48,1024]{1,0:T(8,128)(2,1)} %copy-done.15, ...), custom_call_target="tpu_custom_call" | custom-call | bytes 1572864 | tf_op jit(solution)/shard_map/sort_pieces/pallas_call | solution.py:184
  33.6 2.6 %collective-permute-start.12 = (bf16[32,1792]{1,0:T(8,128)(2,1)}, bf16[32,1792]{1,0:T(8,128)(2,1)S(1)}, u32[]{:S(2)}, u32[]{:S(2)}) collective-permute-start(bf16[32,1792]{1,0:T(8,128)(2,1)} %get-tuple-element.114), channel_id=1, source_target_pairs={{0,8},{1,9},{2,10},{3,11},{4,12},{5,13},{6,14},{7,15},{8,0},{9,1},... | collective-permute-start | bytes 344072 | tf_op jit(solution)/shard_map/ppermute | solution.py:398
  39.7 2.3 %collective-permute-start.14 = (bf16[32,1792]{1,0:T(8,128)(2,1)}, bf16[32,1792]{1,0:T(8,128)(2,1)S(1)}, u32[]{:S(2)}, u32[]{:S(2)}) collective-permute-start(bf16[32,1792]{1,0:T(8,128)(2,1)} %get-tuple-element.116), channel_id=1, source_target_pairs={{0,9},{1,8},{2,11},{3,10},{4,13},{5,12},{6,15},{7,14},{8,1},{9,0},... | collective-permute-start | bytes 344072 | tf_op jit(solution)/shard_map/ppermute | solution.py:398
  42.6 2.7 %sort_pieces.2 = (bf16[8,48,1024]{2,1,0:T(8,128)(2,1)}, bf16[4,48,1024]{2,1,0:T(8,128)(2,1)}, bf16[1,48,1024]{2,1,0:T(8,128)(2,1)S(1)}, bf16[3,48,1024]{2,1,0:T(8,128)(2,1)S(1)}) custom-call(s32[1]{0:T(128)} %bitcast.me_ref, s32[16]{0:T(128)} %perm_ref.9, bf16[48,1024]{1,0:T(8,128)(2,1)} %get-tuple-element.123.refs_0_, bf16[48,1024]{1,0:T(8,128)(2,1)} %copy-done.11, ...), custom_call_target="tpu_custom_call" | custom-call | bytes 1572864 | tf_op jit(solution)/shard_map/sort_pieces/pallas_call | solution.py:184
  46.8 4.3 %collective-permute-done.12.refs_1_ = bf16[32,1792]{1,0:T(8,128)(2,1)S(1)} collective-permute-done((bf16[32,1792]{1,0:T(8,128)(2,1)}, bf16[32,1792]{1,0:T(8,128)(2,1)S(1)}, u32[]{:S(2)}, u32[]{:S(2)}) %collective-permute-start.12) | collective-permute-done | bytes 114720 | tf_op jit(solution)/shard_map/ppermute | solution.py:398
  51.1 3.8 %collective-permute-start.16 = (bf16[32,1792]{1,0:T(8,128)(2,1)S(1)}, bf16[32,1792]{1,0:T(8,128)(2,1)S(1)}, u32[]{:S(2)}, u32[]{:S(2)}) collective-permute-start(bf16[32,1792]{1,0:T(8,128)(2,1)S(1)} %copy-done.33), channel_id=1, source_target_pairs={{0,10},{1,11},{2,8},{3,9},{4,14},{5,15},{6,12},{7,13},{8,2},{9,3},... | collective-permute-start | bytes 344072 | tf_op jit(solution)/shard_map/ppermute | solution.py:398
  54.9 19.8 %collective-permute-done.14.refs_3_ = bf16[32,1792]{1,0:T(8,128)(2,1)S(1)} collective-permute-done((bf16[32,1792]{1,0:T(8,128)(2,1)}, bf16[32,1792]{1,0:T(8,128)(2,1)S(1)}, u32[]{:S(2)}, u32[]{:S(2)}) %collective-permute-start.14) | collective-permute-done | bytes 114720 | tf_op jit(solution)/shard_map/ppermute | solution.py:398
  74.8 4.2 %collective-permute-start.18 = (bf16[32,1792]{1,0:T(8,128)(2,1)S(1)}, bf16[32,1792]{1,0:T(8,128)(2,1)S(1)}, u32[]{:S(2)}, u32[]{:S(2)}) collective-permute-start(bf16[32,1792]{1,0:T(8,128)(2,1)S(1)} %copy-done.31), channel_id=1, source_target_pairs={{0,11},{1,10},{2,9},{3,8},{4,15},{5,14},{6,13},{7,12},{8,3},{9,2},... | collective-permute-start | bytes 344072 | tf_op jit(solution)/shard_map/ppermute | solution.py:398
  79.1 10.5 %collective-permute-done.16.refs_5_ = bf16[32,1792]{1,0:T(8,128)(2,1)S(1)} collective-permute-done((bf16[32,1792]{1,0:T(8,128)(2,1)S(1)}, bf16[32,1792]{1,0:T(8,128)(2,1)S(1)}, u32[]{:S(2)}, u32[]{:S(2)}) %collective-permute-start.16) | collective-permute-done | bytes 114720 | tf_op jit(solution)/shard_map/ppermute | solution.py:398
  89.6 3.4 %collective-permute-start.11 = (bf16[32,1792]{1,0:T(8,128)(2,1)S(1)}, bf16[32,1792]{1,0:T(8,128)(2,1)S(1)}, u32[]{:S(2)}, u32[]{:S(2)}) collective-permute-start(bf16[32,1792]{1,0:T(8,128)(2,1)S(1)} %copy-done.29), channel_id=1, source_target_pairs={{0,15},{1,14},{2,13},{3,12},{4,11},{5,10},{6,9},{7,8},{8,7},{9,6},... | collective-permute-start | bytes 344072 | tf_op jit(solution)/shard_map/ppermute | solution.py:398
  93.0 1.7 %collective-permute-start.5 = (bf16[32,1792]{1,0:T(8,128)(2,1)}, bf16[32,1792]{1,0:T(8,128)(2,1)S(1)}, u32[]{:S(2)}, u32[]{:S(2)}) collective-permute-start(bf16[32,1792]{1,0:T(8,128)(2,1)} %get-tuple-element.106), channel_id=1, source_target_pairs={{0,12},{1,13},{2,14},{3,15},{4,8},{5,9},{6,10},{7,11},{8,4},{9,5},... | collective-permute-start | bytes 344072 | tf_op jit(solution)/shard_map/ppermute | solution.py:398
  94.7 2.6 %collective-permute-done.11.refs_7_ = bf16[32,1792]{1,0:T(8,128)(2,1)S(1)} collective-permute-done((bf16[32,1792]{1,0:T(8,128)(2,1)S(1)}, bf16[32,1792]{1,0:T(8,128)(2,1)S(1)}, u32[]{:S(2)}, u32[]{:S(2)}) %collective-permute-start.11) | collective-permute-done | bytes 114720 | tf_op jit(solution)/shard_map/ppermute | solution.py:398
  98.4 1.6 collective-permute-done.4.refs_0_
  102.5 2.4 %collective-permute-start.9 = (bf16[32,1792]{1,0:T(8,128)(2,1)}, bf16[32,1792]{1,0:T(8,128)(2,1)S(1)}, u32[]{:S(2)}, u32[]{:S(2)}) collective-permute-start(bf16[32,1792]{1,0:T(8,128)(2,1)} %get-tuple-element.110), channel_id=1, source_target_pairs={{0,14},{1,15},{2,12},{3,13},{4,10},{5,11},{6,8},{7,9},{8,6},{9,7},... | collective-permute-start | bytes 344072 | tf_op jit(solution)/shard_map/ppermute | solution.py:398
  105.9 2.6 %join_pieces.3 = (bf16[48,1024]{1,0:T(8,128)(2,1)}, bf16[48,1024]{1,0:T(8,128)(2,1)}, bf16[48,1024]{1,0:T(8,128)(2,1)}, bf16[48,1024]{1,0:T(8,128)(2,1)}, bf16[4...) custom-call(s32[1]{0:T(128)} %bitcast.me_ref, ...), custom_call_target="tpu_custom_call" | custom-call | bytes 1572864 | tf_op jit(solution)/shard_map/join_pieces/pallas_call | solution.py:225
  108.6 2.7 %join_pieces.2 = (bf16[48,1024]{1,0:T(8,128)(2,1)}, bf16[48,1024]{1,0:T(8,128)(2,1)}, bf16[48,1024]{1,0:T(8,128)(2,1)}, bf16[48,1024]{1,0:T(8,128)(2,1)}, bf16[4...) custom-call(s32[1]{0:T(128)} %bitcast.me_ref, ...), custom_call_target="tpu_custom_call" | custom-call | bytes 1572864 | tf_op jit(solution)/shard_map/join_pieces/pallas_call | solution.py:225
  119.0 2.4 %collective-permute-done.28.refs_1_ = bf16[48,1024]{1,0:T(8,128)(2,1)S(1)} collective-permute-done((bf16[48,1024]{1,0:T(8,128)(2,1)}, bf16[48,1024]{1,0:T(8,128)(2,1)S(1)}, u32[]{:S(2)}, u32[]{:S(2)}) %collective-permute-start.28) | collective-permute-done | bytes 98336 | tf_op jit(solution)/shard_map/ppermute | solution.py:398
  127.9 6.0 %collective-permute-done.33.refs_6_ = bf16[48,1024]{1,0:T(8,128)(2,1)S(1)} collective-permute-done((bf16[48,1024]{1,0:T(8,128)(2,1)}, bf16[48,1024]{1,0:T(8,128)(2,1)S(1)}, u32[]{:S(2)}, u32[]{:S(2)}) %collective-permute-start.33) | collective-permute-done | bytes 98336 | tf_op jit(solution)/shard_map/ppermute | solution.py:398
  134.7 3.6 %orthogonal.1 = (bf16[384,1024]{1,0:T(8,128)(2,1)}, bf16[384,1024]{1,0:T(8,128)(2,1)S(1)}) custom-call(s32[1]{0:T(128)} %bitcast.me_ref, f32[384,1024]{1,0:T(8,128)S(1)} %get-tuple-element.122.grad_ref, bf16[48,1024]{1,0:T(8,128)(2,1)S(1)} %copy-done.5, bf16[48,1024]{1,0:T(8,128)(2,1)S(1)} %collective-permute-done.28.refs_1_, ...), custom_call_target="tpu_custom_call" | custom-call | flops 1434451968 | bytes 3932160 | tf_op jit(solution)/shard_map/orthogonal/pallas_call | solution.py:301
  143.6 2.9 %collective-permute-start.53 = (bf16[32,1024]{1,0:T(8,128)(2,1)S(1)}, bf16[32,1024]{1,0:T(8,128)(2,1)S(1)}, u32[]{:S(2)}, u32[]{:S(2)}) collective-permute-start(bf16[32,1024]{1,0:T(8,128)(2,1)S(1)} %get-tuple-element.175), channel_id=1, source_target_pairs={{0,10},{1,11},{2,8},{3,9},{4,14},{5,15},{6,12},{7,13},{8,2},{9,3},... | collective-permute-start | bytes 196616 | tf_op jit(solution)/shard_map/ppermute | solution.py:398
  148.8 3.3 %collective-permute-done.51.refs_2_ = bf16[32,1024]{1,0:T(8,128)(2,1)S(1)} collective-permute-done((bf16[32,1024]{1,0:T(8,128)(2,1)S(1)}, bf16[32,1024]{1,0:T(8,128)(2,1)S(1)}, u32[]{:S(2)}, u32[]{:S(2)}) %collective-permute-start.51) | collective-permute-done | bytes 65568 | tf_op jit(solution)/shard_map/ppermute | solution.py:398
  152.1 2.4 %collective-permute-start.56 = (bf16[32,1024]{1,0:T(8,128)(2,1)S(1)}, bf16[32,1024]{1,0:T(8,128)(2,1)S(1)}, u32[]{:S(2)}, u32[]{:S(2)}) collective-permute-start(bf16[32,1024]{1,0:T(8,128)(2,1)S(1)} %get-tuple-element.178), channel_id=1, source_target_pairs={{0,12},{1,13},{2,14},{3,15},{4,8},{5,9},{6,10},{7,11},{8,4},{9,5},... | collective-permute-start | bytes 196616 | tf_op jit(solution)/shard_map/ppermute | solution.py:398
  155.7 2.6 %collective-permute-start.59 = (bf16[32,1024]{1,0:T(8,128)(2,1)S(1)}, bf16[32,1024]{1,0:T(8,128)(2,1)S(1)}, u32[]{:S(2)}, u32[]{:S(2)}) collective-permute-start(bf16[32,1024]{1,0:T(8,128)(2,1)S(1)} %get-tuple-element.181), channel_id=1, source_target_pairs={{0,14},{1,15},{2,12},{3,13},{4,10},{5,11},{6,8},{7,9},{8,6},{9,7},... | collective-permute-start | bytes 196616 | tf_op jit(solution)/shard_map/ppermute | solution.py:398
  158.3 1.9 %collective-permute-start.60 = (bf16[32,1024]{1,0:T(8,128)(2,1)S(1)}, bf16[32,1024]{1,0:T(8,128)(2,1)S(1)}, u32[]{:S(2)}, u32[]{:S(2)}) collective-permute-start(bf16[32,1024]{1,0:T(8,128)(2,1)S(1)} %get-tuple-element.182), channel_id=1, source_target_pairs={{0,15},{1,14},{2,13},{3,12},{4,11},{5,10},{6,9},{7,8},{8,7},{9,6},... | collective-permute-start | bytes 196616 | tf_op jit(solution)/shard_map/ppermute | solution.py:398
  163.0 2.5 %collective-permute-done.60.refs_11_ = bf16[32,1024]{1,0:T(8,128)(2,1)S(1)} collective-permute-done((bf16[32,1024]{1,0:T(8,128)(2,1)S(1)}, bf16[32,1024]{1,0:T(8,128)(2,1)S(1)}, u32[]{:S(2)}, u32[]{:S(2)}) %collective-permute-start.60) | collective-permute-done | bytes 65568 | tf_op jit(solution)/shard_map/ppermute | solution.py:398
  (189 shorter events, 50.2 us)
Async XLA Ops:
  7.1 10.7 %collective-permute-start.35 = (bf16[48,1024]{1,0:T(8,128)(2,1)}, bf16[48,1024]{1,0:T(8,128)(2,1)S(1)}, u32[]{:S(2)}, u32[]{:S(2)}) collective-permute-start(bf16[48,1024]{1,0:T(8,128)(2,1)} %get-tuple-element.148), channel_id=1, source_target_pairs={{0,4},{1,5},{2,6},{3,7},{4,0},{5,1},{6,2},{7,3},{8,12},{9,13},{10,... | collective-permute-start | bytes 294920 | tf_op jit(solution)/shard_map/ppermute | solution.py:398
  11.9 9.2 %collective-permute-start.38 = (bf16[48,1024]{1,0:T(8,128)(2,1)}, bf16[48,1024]{1,0:T(8,128)(2,1)S(1)}, u32[]{:S(2)}, u32[]{:S(2)}) collective-permute-start(bf16[48,1024]{1,0:T(8,128)(2,1)} %get-tuple-element.151), channel_id=1, source_target_pairs={{0,6},{1,7},{2,4},{3,5},{4,2},{5,3},{6,0},{7,1},{8,14},{9,15},{10,... | collective-permute-start | bytes 294920 | tf_op jit(solution)/shard_map/ppermute | solution.py:398
  19.4 12.9 %collective-permute-start.19 = (bf16[48,1024]{1,0:T(8,128)(2,1)}, bf16[48,1024]{1,0:T(8,128)(2,1)S(1)}, u32[]{:S(2)}, u32[]{:S(2)}) collective-permute-start(bf16[48,1024]{1,0:T(8,128)(2,1)} %get-tuple-element.124), channel_id=1, source_target_pairs={{0,4},{1,5},{2,6},{3,7},{4,0},{5,1},{6,2},{7,3},{8,12},{9,13},{10,... | collective-permute-start | bytes 294920 | tf_op jit(solution)/shard_map/ppermute | solution.py:398
  21.1 11.9 %collective-permute-start.20 = (bf16[48,1024]{1,0:T(8,128)(2,1)}, bf16[48,1024]{1,0:T(8,128)(2,1)S(1)}, u32[]{:S(2)}, u32[]{:S(2)}) collective-permute-start(bf16[48,1024]{1,0:T(8,128)(2,1)} %get-tuple-element.125), channel_id=1, source_target_pairs={{0,5},{1,4},{2,7},{3,6},{4,1},{5,0},{6,3},{7,2},{8,13},{9,12},{10,... | collective-permute-start | bytes 294920 | tf_op jit(solution)/shard_map/ppermute | solution.py:398
  23.1 10.5 %collective-permute-start.21 = (bf16[48,1024]{1,0:T(8,128)(2,1)}, bf16[48,1024]{1,0:T(8,128)(2,1)S(1)}, u32[]{:S(2)}, u32[]{:S(2)}) collective-permute-start(bf16[48,1024]{1,0:T(8,128)(2,1)} %get-tuple-element.126), channel_id=1, source_target_pairs={{0,3},{1,2},{2,1},{3,0},{4,7},{5,6},{6,5},{7,4},{8,11},{9,10},{10,... | collective-permute-start | bytes 294920 | tf_op jit(solution)/shard_map/ppermute | solution.py:398
  25.1 11.1 %collective-permute-start.22 = (bf16[48,1024]{1,0:T(8,128)(2,1)}, bf16[48,1024]{1,0:T(8,128)(2,1)S(1)}, u32[]{:S(2)}, u32[]{:S(2)}) collective-permute-start(bf16[48,1024]{1,0:T(8,128)(2,1)} %get-tuple-element.127), channel_id=1, source_target_pairs={{0,6},{1,7},{2,4},{3,5},{4,2},{5,3},{6,0},{7,1},{8,14},{9,15},{10,... | collective-permute-start | bytes 294920 | tf_op jit(solution)/shard_map/ppermute | solution.py:398
  33.6 17.5 %collective-permute-start.12 = (bf16[32,1792]{1,0:T(8,128)(2,1)}, bf16[32,1792]{1,0:T(8,128)(2,1)S(1)}, u32[]{:S(2)}, u32[]{:S(2)}) collective-permute-start(bf16[32,1792]{1,0:T(8,128)(2,1)} %get-tuple-element.114), channel_id=1, source_target_pairs={{0,8},{1,9},{2,10},{3,11},{4,12},{5,13},{6,14},{7,15},{8,0},{9,1},... | collective-permute-start | bytes 344072 | tf_op jit(solution)/shard_map/ppermute | solution.py:398
  36.2 65.4 %collective-permute-start.42 = (bf16[4,48,1024]{2,1,0:T(8,128)(2,1)}, bf16[4,48,1024]{2,1,0:T(8,128)(2,1)S(1)}, u32[]{:S(2)}, u32[]{:S(2)}) collective-permute-start(bf16[4,48,1024]{2,1,0:T(8,128)(2,1)} %get-tuple-element.156), channel_id=1, source_target_pairs={{0,8},{1,9},{2,10},{3,11},{4,12},{5,13},{6,14},{7,15},{8,0},{9,1},... | collective-permute-start | bytes 1179656 | tf_op jit(solution)/shard_map/ppermute | solution.py:398
  37.6 13.5 %collective-permute-start.13 = (bf16[32,1792]{1,0:T(8,128)(2,1)}, bf16[32,1792]{1,0:T(8,128)(2,1)S(1)}, u32[]{:S(2)}, u32[]{:S(2)}) collective-permute-start(bf16[32,1792]{1,0:T(8,128)(2,1)} %get-tuple-element.115), channel_id=1, source_target_pairs={{0,7},{1,6},{2,5},{3,4},{4,3},{5,2},{6,1},{7,0},{8,15},{9,14},{10,... | collective-permute-start | bytes 344072 | tf_op jit(solution)/shard_map/ppermute | solution.py:398
  39.7 35.1 %collective-permute-start.14 = (bf16[32,1792]{1,0:T(8,128)(2,1)}, bf16[32,1792]{1,0:T(8,128)(2,1)S(1)}, u32[]{:S(2)}, u32[]{:S(2)}) collective-permute-start(bf16[32,1792]{1,0:T(8,128)(2,1)} %get-tuple-element.116), channel_id=1, source_target_pairs={{0,9},{1,8},{2,11},{3,10},{4,13},{5,12},{6,15},{7,14},{8,1},{9,0},... | collective-permute-start | bytes 344072 | tf_op jit(solution)/shard_map/ppermute | solution.py:398
  45.3 29.5 %collective-permute-start.15 = (bf16[32,1792]{1,0:T(8,128)(2,1)S(1)}, bf16[32,1792]{1,0:T(8,128)(2,1)S(1)}, u32[]{:S(2)}, u32[]{:S(2)}) collective-permute-start(bf16[32,1792]{1,0:T(8,128)(2,1)S(1)} %copy-done.34), channel_id=1, source_target_pairs={{0,6},{1,7},{2,4},{3,5},{4,2},{5,3},{6,0},{7,1},{8,14},{9,15},{10,... | collective-permute-start | bytes 344072 | tf_op jit(solution)/shard_map/ppermute | solution.py:398
  51.1 51.4 %collective-permute-start.26 = (bf16[4,48,1024]{2,1,0:T(8,128)(2,1)}, bf16[4,48,1024]{2,1,0:T(8,128)(2,1)S(1)}, u32[]{:S(2)}, u32[]{:S(2)}) collective-permute-start(bf16[4,48,1024]{2,1,0:T(8,128)(2,1)} %get-tuple-element.132), channel_id=1, source_target_pairs={{0,8},{1,9},{2,10},{3,11},{4,12},{5,13},{6,14},{7,15},{8,0},{9,1},... | collective-permute-start | bytes 1179656 | tf_op jit(solution)/shard_map/ppermute | solution.py:398
  51.1 38.4 %collective-permute-start.16 = (bf16[32,1792]{1,0:T(8,128)(2,1)S(1)}, bf16[32,1792]{1,0:T(8,128)(2,1)S(1)}, u32[]{:S(2)}, u32[]{:S(2)}) collective-permute-start(bf16[32,1792]{1,0:T(8,128)(2,1)S(1)} %copy-done.33), channel_id=1, source_target_pairs={{0,10},{1,11},{2,8},{3,9},{4,14},{5,15},{6,12},{7,13},{8,2},{9,3},... | collective-permute-start | bytes 344072 | tf_op jit(solution)/shard_map/ppermute | solution.py:398
  74.8 14.8 %collective-permute-start.17 = (bf16[32,1792]{1,0:T(8,128)(2,1)S(1)}, bf16[32,1792]{1,0:T(8,128)(2,1)S(1)}, u32[]{:S(2)}, u32[]{:S(2)}) collective-permute-start(bf16[32,1792]{1,0:T(8,128)(2,1)S(1)} %copy-done.32), channel_id=1, source_target_pairs={{0,5},{1,4},{2,7},{3,6},{4,1},{5,0},{6,3},{7,2},{8,13},{9,12},{10,... | collective-permute-start | bytes 344072 | tf_op jit(solution)/shard_map/ppermute | solution.py:398
  74.8 18.1 %collective-permute-start.18 = (bf16[32,1792]{1,0:T(8,128)(2,1)S(1)}, bf16[32,1792]{1,0:T(8,128)(2,1)S(1)}, u32[]{:S(2)}, u32[]{:S(2)}) collective-permute-start(bf16[32,1792]{1,0:T(8,128)(2,1)S(1)} %copy-done.31), channel_id=1, source_target_pairs={{0,11},{1,10},{2,9},{3,8},{4,15},{5,14},{6,13},{7,12},{8,3},{9,2},... | collective-permute-start | bytes 344072 | tf_op jit(solution)/shard_map/ppermute | solution.py:398
  93.0 18.4 %collective-permute-start.5 = (bf16[32,1792]{1,0:T(8,128)(2,1)}, bf16[32,1792]{1,0:T(8,128)(2,1)S(1)}, u32[]{:S(2)}, u32[]{:S(2)}) collective-permute-start(bf16[32,1792]{1,0:T(8,128)(2,1)} %get-tuple-element.106), channel_id=1, source_target_pairs={{0,12},{1,13},{2,14},{3,15},{4,8},{5,9},{6,10},{7,11},{8,4},{9,5},... | collective-permute-start | bytes 344072 | tf_op jit(solution)/shard_map/ppermute | solution.py:398
  97.3 14.2 %collective-permute-start.6 = (bf16[32,1792]{1,0:T(8,128)(2,1)}, bf16[32,1792]{1,0:T(8,128)(2,1)S(1)}, u32[]{:S(2)}, u32[]{:S(2)}) collective-permute-start(bf16[32,1792]{1,0:T(8,128)(2,1)} %get-tuple-element.107), channel_id=1, source_target_pairs={{0,3},{1,2},{2,1},{3,0},{4,7},{5,6},{6,5},{7,4},{8,11},{9,10},{10,... | collective-permute-start | bytes 344072 | tf_op jit(solution)/shard_map/ppermute | solution.py:398
  100.0 12.8 %collective-permute-start.7 = (bf16[32,1792]{1,0:T(8,128)(2,1)}, bf16[32,1792]{1,0:T(8,128)(2,1)S(1)}, u32[]{:S(2)}, u32[]{:S(2)}) collective-permute-start(bf16[32,1792]{1,0:T(8,128)(2,1)} %get-tuple-element.108), channel_id=1, source_target_pairs={{0,13},{1,12},{2,15},{3,14},{4,9},{5,8},{6,11},{7,10},{8,5},{9,4},... | collective-permute-start | bytes 344072 | tf_op jit(solution)/shard_map/ppermute | solution.py:398
  101.6 12.0 %collective-permute-start.8 = (bf16[32,1792]{1,0:T(8,128)(2,1)}, bf16[32,1792]{1,0:T(8,128)(2,1)S(1)}, u32[]{:S(2)}, u32[]{:S(2)}) collective-permute-start(bf16[32,1792]{1,0:T(8,128)(2,1)} %get-tuple-element.109), channel_id=1, source_target_pairs={{0,2},{1,3},{2,0},{3,1},{4,6},{5,7},{6,4},{7,5},{8,10},{9,11},{10,... | collective-permute-start | bytes 344072 | tf_op jit(solution)/shard_map/ppermute | solution.py:398
  102.5 12.5 %collective-permute-start.9 = (bf16[32,1792]{1,0:T(8,128)(2,1)}, bf16[32,1792]{1,0:T(8,128)(2,1)S(1)}, u32[]{:S(2)}, u32[]{:S(2)}) collective-permute-start(bf16[32,1792]{1,0:T(8,128)(2,1)} %get-tuple-element.110), channel_id=1, source_target_pairs={{0,14},{1,15},{2,12},{3,13},{4,10},{5,11},{6,8},{7,9},{8,6},{9,7},... | collective-permute-start | bytes 344072 | tf_op jit(solution)/shard_map/ppermute | solution.py:398
  115.0 9.2 %collective-permute-start.30 = (bf16[48,1024]{1,0:T(8,128)(2,1)}, bf16[48,1024]{1,0:T(8,128)(2,1)S(1)}, u32[]{:S(2)}, u32[]{:S(2)}) collective-permute-start(bf16[48,1024]{1,0:T(8,128)(2,1)} %get-tuple-element.139), channel_id=1, source_target_pairs={{0,3},{1,2},{2,1},{3,0},{4,7},{5,6},{6,5},{7,4},{8,11},{9,10},{10,... | collective-permute-start | bytes 294920 | tf_op jit(solution)/shard_map/ppermute | solution.py:398
  117.2 9.3 %collective-permute-start.31 = (bf16[48,1024]{1,0:T(8,128)(2,1)}, bf16[48,1024]{1,0:T(8,128)(2,1)S(1)}, u32[]{:S(2)}, u32[]{:S(2)}) collective-permute-start(bf16[48,1024]{1,0:T(8,128)(2,1)} %get-tuple-element.140), channel_id=1, source_target_pairs={{0,6},{1,7},{2,4},{3,5},{4,2},{5,3},{6,0},{7,1},{8,14},{9,15},{10,... | collective-permute-start | bytes 294920 | tf_op jit(solution)/shard_map/ppermute | solution.py:398
  117.4 9.2 %collective-permute-start.32 = (bf16[48,1024]{1,0:T(8,128)(2,1)}, bf16[48,1024]{1,0:T(8,128)(2,1)S(1)}, u32[]{:S(2)}, u32[]{:S(2)}) collective-permute-start(bf16[48,1024]{1,0:T(8,128)(2,1)} %get-tuple-element.141), channel_id=1, source_target_pairs={{0,7},{1,6},{2,5},{3,4},{4,3},{5,2},{6,1},{7,0},{8,15},{9,14},{10,... | collective-permute-start | bytes 294920 | tf_op jit(solution)/shard_map/ppermute | solution.py:398
  121.4 12.6 %collective-permute-start.33 = (bf16[48,1024]{1,0:T(8,128)(2,1)}, bf16[48,1024]{1,0:T(8,128)(2,1)S(1)}, u32[]{:S(2)}, u32[]{:S(2)}) collective-permute-start(bf16[48,1024]{1,0:T(8,128)(2,1)} %get-tuple-element.142), channel_id=1, source_target_pairs={{0,2},{1,3},{2,0},{3,1},{4,6},{5,7},{6,4},{7,5},{8,10},{9,11},{10,... | collective-permute-start | bytes 294920 | tf_op jit(solution)/shard_map/ppermute | solution.py:398
  122.7 12.0 %collective-permute-start.34 = (bf16[48,1024]{1,0:T(8,128)(2,1)}, bf16[48,1024]{1,0:T(8,128)(2,1)S(1)}, u32[]{:S(2)}, u32[]{:S(2)}) collective-permute-start(bf16[48,1024]{1,0:T(8,128)(2,1)} %get-tuple-element.143), channel_id=1, source_target_pairs={{0,1},{1,0},{2,3},{3,2},{4,5},{5,4},{6,7},{7,6},{8,9},{9,8},{10,11... | collective-permute-start | bytes 294920 | tf_op jit(solution)/shard_map/ppermute | solution.py:398
  124.2 14.1 %collective-permute-start.45 = (bf16[48,1024]{1,0:T(8,128)(2,1)S(1)}, bf16[48,1024]{1,0:T(8,128)(2,1)S(1)}, u32[]{:S(2)}, u32[]{:S(2)}) collective-permute-start(bf16[48,1024]{1,0:T(8,128)(2,1)S(1)} %copy-done.39), channel_id=1, source_target_pairs={{0,3},{1,2},{2,1},{3,0},{4,7},{5,6},{6,5},{7,4},{8,11},{9,10},{10,... | collective-permute-start | bytes 294920 | tf_op jit(solution)/shard_map/ppermute | solution.py:398
  126.4 11.9 %collective-permute-start.46 = (bf16[48,1024]{1,0:T(8,128)(2,1)S(1)}, bf16[48,1024]{1,0:T(8,128)(2,1)S(1)}, u32[]{:S(2)}, u32[]{:S(2)}) collective-permute-start(bf16[48,1024]{1,0:T(8,128)(2,1)S(1)} %copy-done.38), channel_id=1, source_target_pairs={{0,6},{1,7},{2,4},{3,5},{4,2},{5,3},{6,0},{7,1},{8,14},{9,15},{10,... | collective-permute-start | bytes 294920 | tf_op jit(solution)/shard_map/ppermute | solution.py:398
  126.6 11.7 %collective-permute-start.47 = (bf16[48,1024]{1,0:T(8,128)(2,1)S(1)}, bf16[48,1024]{1,0:T(8,128)(2,1)S(1)}, u32[]{:S(2)}, u32[]{:S(2)}) collective-permute-start(bf16[48,1024]{1,0:T(8,128)(2,1)S(1)} %copy-done.37), channel_id=1, source_target_pairs={{0,7},{1,6},{2,5},{3,4},{4,3},{5,2},{6,1},{7,0},{8,15},{9,14},{10,... | collective-permute-start | bytes 294920 | tf_op jit(solution)/shard_map/ppermute | solution.py:398
  141.2 10.9 %collective-permute-start.51 = (bf16[32,1024]{1,0:T(8,128)(2,1)S(1)}, bf16[32,1024]{1,0:T(8,128)(2,1)S(1)}, u32[]{:S(2)}, u32[]{:S(2)}) collective-permute-start(bf16[32,1024]{1,0:T(8,128)(2,1)S(1)} %get-tuple-element.173), channel_id=1, source_target_pairs={{0,9},{1,8},{2,11},{3,10},{4,13},{5,12},{6,15},{7,14},{8,1},{9,0},... | collective-permute-start | bytes 196616 | tf_op jit(solution)/shard_map/ppermute | solution.py:398
  142.7 11.9 %collective-permute-start.52 = (bf16[32,1024]{1,0:T(8,128)(2,1)S(1)}, bf16[32,1024]{1,0:T(8,128)(2,1)S(1)}, u32[]{:S(2)}, u32[]{:S(2)}) collective-permute-start(bf16[32,1024]{1,0:T(8,128)(2,1)S(1)} %get-tuple-element.174), channel_id=1, source_target_pairs={{0,7},{1,6},{2,5},{3,4},{4,3},{5,2},{6,1},{7,0},{8,15},{9,14},{10,... | collective-permute-start | bytes 196616 | tf_op jit(solution)/shard_map/ppermute | solution.py:398
  143.6 11.8 %collective-permute-start.53 = (bf16[32,1024]{1,0:T(8,128)(2,1)S(1)}, bf16[32,1024]{1,0:T(8,128)(2,1)S(1)}, u32[]{:S(2)}, u32[]{:S(2)}) collective-permute-start(bf16[32,1024]{1,0:T(8,128)(2,1)S(1)} %get-tuple-element.175), channel_id=1, source_target_pairs={{0,10},{1,11},{2,8},{3,9},{4,14},{5,15},{6,12},{7,13},{8,2},{9,3},... | collective-permute-start | bytes 196616 | tf_op jit(solution)/shard_map/ppermute | solution.py:398
  148.0 10.3 %collective-permute-start.55 = (bf16[32,1024]{1,0:T(8,128)(2,1)S(1)}, bf16[32,1024]{1,0:T(8,128)(2,1)S(1)}, u32[]{:S(2)}, u32[]{:S(2)}) collective-permute-start(bf16[32,1024]{1,0:T(8,128)(2,1)S(1)} %get-tuple-element.177), channel_id=1, source_target_pairs={{0,6},{1,7},{2,4},{3,5},{4,2},{5,3},{6,0},{7,1},{8,14},{9,15},{10,... | collective-permute-start | bytes 196616 | tf_op jit(solution)/shard_map/ppermute | solution.py:398
  (71 other events, 943.7 us)
